TPU v7x, 32 devices: a whole 2x2x4 slice. The times are simulated.
32 devices in a mesh: expert: 8 (over z, y), shard: 4 (over x, core).
Axes of the slice: x: 2, y: 2, z: 4, core: 2. Of those that a mesh axis runs over, the one named last changes fastest.
Arguments:
- tokens: bfloat16 [16384, 768], P(('expert', 'shard')), may hold values from -6 to 6
- segment_ids: int32 [16384], P(('expert', 'shard')), may hold values from 0 to 1, as said below
- routes: int32 [16384], P(('expert', 'shard')), may hold values from 0 to 7, as said below
- slots: int32 [16384], P(('expert', 'shard')), may hold values from 0 to 127, as said below
- qkv_weight: bfloat16 [768, 2304], P('shard'), may hold values from -0.21875 to 0.21875
- out_weight: bfloat16 [768, 768], P('shard'), may hold values from -1.25 to 1.25
- bias_table: float32 [32, 12], replicated, may hold values from -4 to 4
- norm_gain: float32 [768], replicated, may hold values from 0.1 to 1.9
- ffn_gain: float32 [768], replicated, may hold values from 0.1 to 1.9
- router_weight: float32 [768, 8], replicated, may hold values from -0.15625 to 0.15625
- expert_in: bfloat16 [8, 768, 3072], P('expert'), may hold values from -0.21875 to 0.21875
- expert_out: bfloat16 [8, 3072, 768], P('expert'), may hold values from -0.875 to 0.875
- cotangent: bfloat16 [16384, 768], P(('expert', 'shard')), may hold values from -6 to 6
Outputs:
- layer_out: float32 [16384, 768], P(('expert', 'shard'))
- grad_tokens: float32 [16384, 768], P(('expert', 'shard'))
- grad_qkv: float32 [768, 2304], P(('expert', 'shard'))
- grad_out_weight: float32 [768, 768], P(('expert', 'shard'))
- grad_bias_table: float32 [32, 12], replicated
- grad_norm_gain: float32 [768], replicated
- grad_ffn_gain: float32 [768], replicated
- grad_router: float32 [768, 8], replicated
- grad_expert_in: float32 [8, 768, 3072], P('expert', 'shard')
- grad_expert_out: float32 [8, 3072, 768], P('expert', 'shard')
Inputs may be any that keep to these rules, and one draw needn't show every extreme that they name: `segment_ids`: segment numbers within one device's 512 rows never fall; every number 0 to 1 occurs on every device. `routes`: within one device's 512 rows no expert is named more than 128 times; some expert is named exactly 128 times by every device. Tokens of one device that name the same expert have different slots.
All inputs are finite; a program needn't handle non-finite values.
Results may differ from a plain program's by a relative error of at most 0.014.
Values may be sent and summed in bfloat16 or wider, within the bound.
A program may use at most 192 MiB of HBM per device.

v0:
```python
import math

import jax
import jax.numpy as jnp
from jax import lax
from jax.sharding import PartitionSpec as P

MAXDIST = 128


epsilon = 1e-06
neg_large = -1e30
highest = lax.Precision.HIGHEST


def thresholds(buckets, farthest):
    exact_count = buckets // 4
    return [
        math.ceil(exact_count * (farthest / exact_count) ** (tier_index / exact_count))
        for tier_index in range(1, exact_count)
    ]


def bucket_of(distance, buckets, farthest):
    exact_count = buckets // 4
    magnitude = jnp.abs(distance)
    beyond = exact_count + sum(
        (
            (magnitude >= edge_value).astype(jnp.int32)
            for edge_value in thresholds(buckets, farthest)
        )
    )
    near_far = jnp.where(magnitude < exact_count, magnitude, beyond)
    return jnp.where(distance > 0, 2 * exact_count, 0) + near_far


def relative_bias(table, first_query, query_rows, key_rows):
    buckets = table.shape[0]
    span_width = query_rows + key_rows
    distance = jnp.arange(span_width, dtype=jnp.int32) - (query_rows - 1) - first_query
    one_hot = (
        bucket_of(distance, buckets, MAXDIST)[:, None]
        == jnp.arange(buckets, dtype=jnp.int32)[None, :]
    ).astype(jnp.float32)
    along = jnp.dot(one_hot, table, precision=highest).T
    heads_count = along.shape[0]
    tiled = jnp.broadcast_to(along[:, None, :], (heads_count, query_rows, span_width)).reshape(
        heads_count, query_rows * span_width
    )
    skewed = tiled[:, : query_rows * (span_width - 1)].reshape(
        heads_count, query_rows, span_width - 1
    )
    return skewed[:, :, query_rows - 1 : query_rows - 1 + key_rows]


def normalize(values, gain):
    scale_inv = lax.rsqrt(jnp.mean(values * values, axis=-1, keepdims=True) + epsilon)
    return (values * scale_inv * gain, scale_inv)


def norm_backward(values, scale_inv, gain, upstream):
    scaled = upstream * gain
    inner_mean = jnp.mean(scaled * values, axis=-1, keepdims=True)
    grad_values = scale_inv * scaled - values * scale_inv * scale_inv * scale_inv * inner_mean
    grad_gain = jnp.sum(upstream * values * scale_inv, axis=0)
    return (grad_values, grad_gain)


def gelu_value(values):
    return 0.5 * values * (1.0 + lax.erf(values * 0.7071067811865476))


def gelu_slope(values):
    return (
        0.5 * (1.0 + lax.erf(values * 0.7071067811865476))
        + values * jnp.exp(-0.5 * values * values) * 0.3989422804014327
    )


def contract_rows(left_side, right_side):
    return lax.dot_general(
        left_side, right_side, (((0,), (0,)), ((), ())), preferred_element_type=jnp.float32
    )


def local(
    tokens,
    segment_ids,
    routes,
    slots,
    qkv_weight,
    out_weight,
    bias_table,
    norm_gain,
    ffn_gain,
    router_weight,
    expert_in,
    expert_out,
    cotangent,
):
    token_rows, width = tokens.shape
    heads_count = bias_table.shape[1]
    head_width = width // heads_count
    experts_count = router_weight.shape[1]
    inner_width = expert_in.shape[2]
    capacity = 2 * token_rows // experts_count
    block_rows = min(512, token_rows)
    weight_in = expert_in[0]
    weight_out = expert_out[0]
    full_qkv, full_out = (
        lax.all_gather(qkv_weight, "shard", axis=0, tiled=True),
        lax.all_gather(out_weight, "shard", axis=0, tiled=True),
    )
    inputs = tokens.astype(jnp.float32)
    normed, scale_one = normalize(inputs, norm_gain)
    normed_low = normed.astype(jnp.bfloat16)
    packed = jnp.dot(normed_low, full_qkv, preferred_element_type=jnp.float32).astype(jnp.bfloat16)
    queries = packed[:, :width].reshape(token_rows, heads_count, head_width)
    keys_all = packed[:, width : 2 * width].reshape(token_rows, heads_count, head_width)
    values_all = packed[:, 2 * width :].reshape(token_rows, heads_count, head_width)

    def block_scores(first_query, bias_block):
        allowed = (
            segment_ids[first_query : first_query + block_rows, None] == segment_ids[None, :]
        )[None]
        raw_scores = (
            jnp.einsum("qhd,khd->hqk", queries, keys_all, preferred_element_type=jnp.float32)
            * 0.125
            + bias_block
        )
        return (jnp.where(allowed, raw_scores, neg_large), queries)

    block_index = 0
    first_query = block_index * block_rows
    bias_block = relative_bias(bias_table, first_query, block_rows, token_rows)
    scores, query_block = block_scores(first_query, bias_block)
    largest = jnp.max(scores, axis=-1, keepdims=True)
    exp_scores = jnp.exp(scores - largest)
    totals = jnp.sum(exp_scores, axis=-1, keepdims=True)
    weights_low = (exp_scores / totals).astype(jnp.bfloat16)
    mixed = jnp.einsum("hqk,khd->qhd", weights_low, values_all, preferred_element_type=jnp.float32)
    mixed_blocks = mixed.reshape(block_rows, width).astype(jnp.bfloat16)
    log_totals = [largest + jnp.log(totals)]
    branch = jnp.dot(mixed_blocks, full_out, preferred_element_type=jnp.float32)
    middle = inputs + branch
    normed_two, scale_two = normalize(middle, ffn_gain)
    logits = jnp.dot(normed_two, router_weight, precision=highest)
    router_probs = jax.nn.softmax(logits, axis=-1)
    chosen = (routes[:, None] == jnp.arange(experts_count, dtype=jnp.int32)[None, :]).astype(
        jnp.float32
    )
    gates = jnp.sum(router_probs * chosen, axis=-1)
    sent = normed_two.astype(jnp.bfloat16)
    dest_rows = routes * capacity + slots
    outgoing = (
        jnp.zeros((experts_count * capacity, width), jnp.bfloat16)
        .at[dest_rows]
        .set(sent)
        .reshape(experts_count, capacity, width)
    )
    arrived_rows = lax.all_to_all(outgoing, "expert", split_axis=0, concat_axis=0, tiled=True)
    inner_raw = jnp.dot(
        arrived_rows.reshape(-1, width), weight_in, preferred_element_type=jnp.float32
    )
    activated_rows = gelu_value(inner_raw).astype(jnp.bfloat16)
    result_rows = jnp.dot(activated_rows, weight_out, preferred_element_type=jnp.float32).astype(
        jnp.bfloat16
    )
    dispatched = (
        inner_raw.reshape(arrived_rows.shape[0], arrived_rows.shape[1], inner_width),
        result_rows.reshape(arrived_rows.shape),
    )[1]
    coming_back = lax.all_to_all(
        dispatched, "expert", split_axis=0, concat_axis=0, tiled=True
    ).reshape(experts_count * capacity, width)
    expert_rows = jnp.take(coming_back, dest_rows, axis=0).astype(jnp.float32)
    layer_out = middle + gates[:, None] * expert_rows
    upstream = cotangent.astype(jnp.float32)
    gate_grad = jnp.sum(upstream * expert_rows, axis=-1)
    row_grad = (gates[:, None] * upstream).astype(jnp.bfloat16)
    grad_buffer = (
        jnp.zeros((experts_count * capacity, width), jnp.bfloat16)
        .at[dest_rows]
        .set(row_grad)
        .reshape(experts_count, capacity, width)
    )
    arrived = lax.all_to_all(outgoing, "expert", split_axis=0, concat_axis=0, tiled=True)
    inner_flat = jnp.dot(arrived.reshape(-1, width), weight_in, preferred_element_type=jnp.float32)
    grad_arrived = lax.all_to_all(grad_buffer, "expert", split_axis=0, concat_axis=0, tiled=True)
    flat_in = arrived.reshape(-1, width)
    flat_grad = grad_arrived.reshape(-1, width)
    activated = gelu_value(inner_flat).astype(jnp.bfloat16)
    act_grad = jnp.dot(flat_grad, weight_out.T, preferred_element_type=jnp.float32)
    inner_grad = (act_grad * gelu_slope(inner_flat)).astype(jnp.bfloat16)
    input_grad = (
        jnp.dot(inner_grad, weight_in.T, preferred_element_type=jnp.float32)
        .astype(jnp.bfloat16)
        .reshape(arrived.shape)
    )
    returned_grad = lax.all_to_all(
        input_grad, "expert", split_axis=0, concat_axis=0, tiled=True
    ).reshape(experts_count * capacity, width)
    sent_grad = jnp.take(returned_grad, dest_rows, axis=0).astype(jnp.float32)
    columns = flat_in
    grad_in_rows = lax.psum_scatter(
        contract_rows(columns, inner_grad).astype(jnp.bfloat16),
        "shard",
        scatter_dimension=0,
        tiled=True,
    ).astype(jnp.float32)
    columns = activated
    grad_out_rows = lax.psum_scatter(
        contract_rows(columns, flat_grad).astype(jnp.bfloat16),
        "shard",
        scatter_dimension=0,
        tiled=True,
    ).astype(jnp.float32)
    logit_grad = (gate_grad * gates)[:, None] * (chosen - router_probs)
    router_grad = lax.dot_general(
        normed_two, logit_grad, (((0,), (0,)), ((), ())), precision=highest
    )
    normed_two_grad = jnp.dot(logit_grad, router_weight.T, precision=highest) + sent_grad
    middle_norm_grad, ffn_gain_grad = norm_backward(middle, scale_two, ffn_gain, normed_two_grad)
    middle_grad = upstream + middle_norm_grad
    branch_grad = middle_grad.astype(jnp.bfloat16)
    attended_grad = (
        jnp.dot(branch_grad, full_out.T, preferred_element_type=jnp.float32)
        .astype(jnp.bfloat16)
        .reshape(token_rows, heads_count, head_width)
    )
    block_index = 0
    first_query = block_index * block_rows
    bias_block, bias_pull = jax.vjp(
        lambda table_piece: relative_bias(table_piece, first_query, block_rows, token_rows),
        bias_table,
    )
    scores, query_block = block_scores(first_query, bias_block)
    weights_soft = jnp.exp(scores - log_totals[block_index])
    prob_grad = jnp.einsum(
        "qhd,khd->hqk", attended_grad, values_all, preferred_element_type=jnp.float32
    )
    score_grad = (
        weights_soft * (prob_grad - jnp.sum(weights_soft * prob_grad, axis=-1, keepdims=True))
    ).astype(jnp.bfloat16)
    query_grads = (
        jnp.einsum("hqk,khd->qhd", score_grad, keys_all, preferred_element_type=jnp.float32) * 0.125
    )
    key_grad = (
        jnp.einsum("hqk,qhd->khd", score_grad, query_block, preferred_element_type=jnp.float32)
        * 0.125
    )
    value_grad = jnp.einsum(
        "hqk,qhd->khd",
        weights_soft.astype(jnp.bfloat16),
        attended_grad,
        preferred_element_type=jnp.float32,
    )
    table_grad = bias_pull(score_grad.astype(jnp.float32))[0]
    packed_grad = jnp.concatenate(
        [
            query_grads.reshape(token_rows, width),
            key_grad.reshape(token_rows, width),
            value_grad.reshape(token_rows, width),
        ],
        axis=1,
    ).astype(jnp.bfloat16)
    normed_grad = jnp.dot(packed_grad, full_qkv.T, preferred_element_type=jnp.float32)
    input_norm_grad, norm_gain_grad = norm_backward(inputs, scale_one, norm_gain, normed_grad)
    grad_tokens = middle_grad + input_norm_grad
    grad_weights = lax.psum_scatter(
        jnp.concatenate(
            [contract_rows(normed_low, packed_grad), contract_rows(mixed_blocks, branch_grad)],
            axis=1,
        ),
        ("expert", "shard"),
        scatter_dimension=0,
        tiled=True,
    )
    grad_qkv = grad_weights[:, : 3 * width]
    grad_out_weight = grad_weights[:, 3 * width :]
    table_grad, norm_gain_grad, ffn_gain_grad, router_grad = lax.psum(
        (table_grad, norm_gain_grad, ffn_gain_grad, router_grad), ("expert", "shard")
    )
    return (
        layer_out,
        grad_tokens,
        grad_qkv,
        grad_out_weight,
        table_grad,
        norm_gain_grad,
        ffn_gain_grad,
        router_grad,
        grad_in_rows[None],
        grad_out_rows[None],
    )


def solution(mesh):
    placed = (
        P(("expert", "shard"), None),
        P(("expert", "shard")),
        P(("expert", "shard")),
        P(("expert", "shard")),
        P("shard", None),
        P("shard", None),
        P(),
        P(),
        P(),
        P(),
        P("expert", None, None),
        P("expert", None, None),
        P(("expert", "shard"), None),
    )
    return jax.shard_map(
        local,
        mesh=mesh,
        in_specs=placed,
        out_specs=(
            P(("expert", "shard"), None),
            P(("expert", "shard"), None),
            P(("expert", "shard"), None),
            P(("expert", "shard"), None),
            P(),
            P(),
            P(),
            P(),
            P("expert", "shard", None),
            P("expert", "shard", None),
        ),
        check_vma=False,
    )
```

profile of v0, /device:TPU:0, one launch (start us, length us, event | category | flops | bytes accessed | tf_op | source)
XLA Modules:
  0.0 650.1 jit_solution(12893189999254237881)
XLA Ops:
  12.2 12.7 %broadcast_in_dim.49 = f32[12,512,1024]{2,1,0:T(8,128)} broadcast(f32[12,1024]{1,0:T(8,128)S(1)} %convolution_bitcast_fusion), dimensions={0,2} | broadcast | bytes 25214976 | tf_op jit(solution)/shard_map/broadcast_in_dim | solution.py:47
  24.9 10.9 %pad.17 = f32[16,512,1024]{2,1,0:T(8,128)S(1)} pad(f32[12,512,1024]{2,1,0:T(8,128)} %broadcast_in_dim.49, f32[]{:T(128)} %constant.32.clone.1), padding=0_4x0_0x0_0 | pad | bytes 58720260
  35.8 39.7 %copy.54 = f32[2,8,512,1024]{3,1,2,0:T(8,128)} copy(f32[2,8,512,1024]{3,2,1,0:T(8,128)S(1)} %bitcast.88) | data formatting | bytes 67108864
  75.6 22.6 %slice.37 = f32[12,523776]{1,0:T(8,128)} slice(f32[12,524288]{1,0:T(8,128)} %bitcast.90), slice={[0:12], [0:523776]} | slice | bytes 50282496 | tf_op jit(solution)/shard_map/slice | solution.py:50
  98.1 41.7 %reshape.206 = f32[12,512,1023]{2,1,0:T(8,128)} reshape(f32[12,523776]{1,0:T(8,128)} %slice.37) | data formatting | bytes 50282496 | tf_op jit(solution)/shard_map/reshape | solution.py:50
  139.9 13.4 %slice.38 = f32[12,512,512]{2,1,0:T(8,128)} slice(f32[12,512,1023]{2,1,0:T(8,128)} %reshape.206), slice={[0:12], [0:512], [511:1023]} | slice | bytes 25165824 | tf_op jit(solution)/shard_map/slice | solution.py:53
  153.3 12.7 %copy.52 = f32[12,512,512]{1,2,0:T(8,128)} copy(f32[12,512,512]{2,1,0:T(8,128)} %slice.38) | data formatting | bytes 25165824
  209.2 31.4 %all-to-all-done = bf16[8,128,768]{2,1,0:T(8,128)(2,1)} async-done(((bf16[8,128,768]{2,1,0:T(8,128)(2,1)}), bf16[8,128,768]{2,1,0:T(8,128)(2,1)}, u32[]{:S(2)}, u32[]{:S(2)}) %all-to-all-start) | async-done | bytes 1572896 | tf_op jit(solution)/shard_map/all_to_all | solution.py:161
  244.5 11.3 %multiply_convert_fusion.1 = (bf16[1024,3072]{1,0:T(8,128)(2,1)}, f32[1024,3072]{1,0:T(8,128)}) fusion(bf16[1024,768]{1,0:T(8,128)(2,1)} %bitcast.7, bf16[1,768,3072]{2,1,0:T(8,128)(2,1)} %param.25), kind=kOutput, calls=%fused_computation.16 | convolution fusion | flops 4847566848 | bytes 25165824 | tf_op jit(solution)/shard_map/dot_general | solution.py:162
  255.8 25.7 %all-to-all-done.2 = bf16[8,128,768]{2,1,0:T(8,128)(2,1)S(1)} async-done(((bf16[8,128,768]{2,1,0:T(8,128)(2,1)}), bf16[8,128,768]{2,1,0:T(8,128)(2,1)S(1)}, u32[]{:S(2)}, u32[]{:S(2)}) %all-to-all-start.2) | async-done | bytes 1572896 | tf_op jit(solution)/shard_map/all_to_all | solution.py:189
  281.5 9.7 %convolution_convert_fusion = bf16[3072,768]{1,0:T(8,128)(2,1)} fusion(bf16[1024,3072]{1,0:T(8,128)(2,1)} %get-tuple-element.32, bf16[1024,768]{1,0:T(8,128)(2,1)S(1)} %bitcast.105), kind=kOutput, calls=%fused_computation.27 | convolution fusion | flops 4834197504 | bytes 12582912 | tf_op jit(solution)/shard_map/dot_general | solution.py:81
  291.3 11.8 %fusion.5 = bf16[1024,3072]{1,0:T(8,128)(2,1)S(1)} fusion(f32[1024,3072]{1,0:T(8,128)} %get-tuple-element.33, bf16[1024,768]{1,0:T(8,128)(2,1)S(1)} %bitcast.106, bf16[1,3072,768]{2,1,0:T(8,128)(2,1)} %param.26), kind=kOutput, calls=%fused_computation.12 | convolution fusion | flops 4863295488 | bytes 25165824 | tf_op jit(solution)/shard_map/dot_general | solution.py:193
  303.1 10.8 %fusion.21 = bf16[1024,768]{1,0:T(8,128)(2,1)} fusion(bf16[1024,3072]{1,0:T(8,128)(2,1)S(1)} %fusion.5, bf16[1,768,3072]{2,1,0:T(8,128)(2,1)} %param.25), kind=kOutput, calls=%fused_computation.49 | convolution fusion | flops 4832624640 | bytes 12582912 | tf_op jit(solution)/shard_map/dot_general | solution.py:196
  317.5 9.2 %convolution_convert_fusion.1 = bf16[768,3072]{1,0:T(8,128)(2,1)} fusion(bf16[1024,768]{1,0:T(8,128)(2,1)} %bitcast.7, bf16[1024,3072]{1,0:T(8,128)(2,1)} %copy-done.31), kind=kOutput, calls=%fused_computation.28 | convolution fusion | flops 4834197504 | bytes 12582912 | tf_op jit(solution)/shard_map/dot_general | solution.py:81
  326.7 9.4 %fusion.24 = bf16[1024,768]{1,0:T(8,128)(2,1)} fusion(bf16[1024,3072]{1,0:T(8,128)(2,1)} %get-tuple-element.32, bf16[1,3072,768]{2,1,0:T(8,128)(2,1)} %param.26), kind=kOutput, calls=%fused_computation.50 | convolution fusion | flops 4832624640 | bytes 12582912 | tf_op jit(solution)/shard_map/dot_general | solution.py:166
  336.1 18.4 %all-to-all-done.3 = bf16[8,128,768]{2,1,0:T(8,128)(2,1)S(1)} async-done(((bf16[8,128,768]{2,1,0:T(8,128)(2,1)}), bf16[8,128,768]{2,1,0:T(8,128)(2,1)S(1)}, u32[]{:S(2)}, u32[]{:S(2)}) %all-to-all-start.3) | async-done | bytes 1572896 | tf_op jit(solution)/shard_map/all_to_all | solution.py:200
  362.0 33.4 %all-to-all-done.1 = bf16[8,128,768]{2,1,0:T(8,128)(2,1)} async-done(((bf16[8,128,768]{2,1,0:T(8,128)(2,1)}), bf16[8,128,768]{2,1,0:T(8,128)(2,1)}, u32[]{:S(2)}, u32[]{:S(2)}) %all-to-all-start.1) | async-done | bytes 1572896 | tf_op jit(solution)/shard_map/all_to_all | solution.py:173
  430.9 10.6 %pad.8.clone = bf16[12,512,1023]{2,1,0:T(8,128)(2,1)} pad(bf16[12,512,512]{2,1,0:T(8,128)(2,1)} %copy.53, bf16[]{:T(256)} %constant.20.clone.1), padding=0_0x0_0x511_0 | pad | bytes 18862082 | tf_op jit(solution)/shard_map/transpose(jvp())/pad | solution.py:53
  441.5 35.1 %reshape.219 = bf16[12,523776]{1,0:T(8,128)(2,1)} reshape(bf16[12,512,1023]{2,1,0:T(8,128)(2,1)} %pad.8.clone) | data formatting | bytes 25141248 | tf_op jit(solution)/shard_map/transpose(jvp())/reshape | solution.py:50
  505.1 8.8 %pad_convert_fusion = f32[12,524288]{1,0:T(8,128)S(1)} fusion(bf16[12,523776]{1,0:T(8,128)(2,1)} %reshape.219), kind=kLoop, calls=%fused_computation.6 | loop fusion | flops 6291456 | bytes 37736448 | tf_op jit(solution)/shard_map/transpose(jvp())/reshape | solution.py:47
  513.8 35.7 %copy.55 = f32[2,8,512,1024]{3,2,1,0:T(8,128)} copy(f32[2,8,512,1024]{3,1,2,0:T(8,128)S(1)} %bitcast.89) | data formatting | bytes 67108864
  549.5 11.3 %slice_reduce_fusion = f32[12,1024]{1,0:T(8,128)S(1)} fusion(f32[16,512,1024]{2,1,0:T(8,128)} %bitcast.91), kind=kLoop, calls=%fused_computation.4 | loop fusion | flops 6279168 | bytes 25214976 | tf_op jit(solution)/shard_map/transpose(jvp())/reduce_sum | solution.py:47
  565.8 39.5 %all-reduce.2 = (f32[32,12]{0,1:T(8,128)}, f32[768]{0:T(1024)}, f32[768]{0:T(1024)}, f32[768,8]{0,1:T(8,128)}) all-reduce(f32[32,12]{0,1:T(8,128)S(1)} %fusion.61, f32[768]{0:T(1024)S(1)} %get-tuple-element.13, f32[768]{0:T(1024)S(1)} %get-tuple-element.11, ...), channel_id=1, replica_groups=mesh['expert'=8,'shard'=4] {'expert','shard'}, use_global_device_ids=true, to_apply=%region_15.17 | all-reduce | flops 8064 | bytes 64512 | tf_op jit(solution)/shard_map/psum | solution.py:281
  614.2 25.8 %reduce-scatter.4.cloned.1.call-done = f32[24,3072]{1,0:T(8,128)} async-done(((f32[768,3072]{1,0:T(8,128)}), f32[24,3072]{1,0:T(8,128)}) %reduce-scatter.4.cloned.1.call-update) | async-done | bytes 294928 | tf_op jit(solution)/shard_map/reduce_scatter | solution.py:270
  (146 shorter events, 143.7 us)
Async XLA Ops:
  7.2 196.5 %copy-start = (f32[768,8]{0,1:T(8,128)S(1)}, f32[768,8]{0,1:T(8,128)}, u32[]{:S(2)}) copy-start(f32[768,8]{0,1:T(8,128)} %param.24) | copy-start | bytes 73732
  7.2 158.8 %all-gather.3.cloned.1.call-start = ((), (), s32[]{:S(2)}) async-start(), calls=%async_computation.7 | async-start | bytes 4423680 | tf_op jit(solution)/shard_map/all_gather | solution.py:111
  7.9 181.7 %all-gather.5.cloned.1.call-start = ((), (), s32[]{:S(2)}) async-start(), calls=%async_computation.8 | async-start | bytes 1474560 | tf_op jit(solution)/shard_map/all_gather | solution.py:112
  8.7 16.2 %copy-start.25 = (s32[1024]{0:T(1024)}, s32[1024]{0:T(1024)S(1)}, u32[]{:S(2)}) copy-start(s32[1024]{0:T(1024)S(1)} %fusion.75) | copy-start | bytes 12292
  153.3 12.7 %copy-start.24 = (s32[512]{0:T(512)S(1)}, s32[512]{0:T(512)}, u32[]{:S(2)}) copy-start(s32[512]{0:T(512)} %param.17) | copy-start | bytes 6148
  153.3 12.7 %copy-start.28 = (s32[512]{0:T(512)S(1)}, s32[512]{0:T(512)}, u32[]{:S(2)}) copy-start(s32[512]{0:T(512)} %param.18) | copy-start | bytes 6148
  153.3 12.7 %copy-start.14 = (bf16[512,768]{1,0:T(8,128)(2,1)S(1)}, bf16[512,768]{1,0:T(8,128)(2,1)}, u32[]{:S(2)}) copy-start(bf16[512,768]{1,0:T(8,128)(2,1)} %param.15) | copy-start | bytes 2359300
  153.3 12.7 %copy-start.27 = (f32[768]{0:T(1024)S(1)}, f32[768]{0:T(1024)}, u32[]{:S(2)}) copy-start(f32[768]{0:T(1024)} %param.22) | copy-start | bytes 9220
  192.1 211.0 %copy-start.2 = (f32[512,768]{1,0:T(8,128)}, f32[512,768]{1,0:T(8,128)S(1)}, u32[]{:S(2)}) copy-start(f32[512,768]{1,0:T(8,128)S(1)} %get-tuple-element.29) | copy-start | bytes 4718596
  196.1 44.6 %all-to-all-start = ((bf16[8,128,768]{2,1,0:T(8,128)(2,1)}), bf16[8,128,768]{2,1,0:T(8,128)(2,1)}, u32[]{:S(2)}, u32[]{:S(2)}) async-start(bf16[8,128,768]{2,1,0:T(8,128)(2,1)} %bitcast.100), calls=%async_computation | async-start | bytes 3145728 | tf_op jit(solution)/shard_map/all_to_all | solution.py:161
  240.7 40.8 %all-to-all-start.2 = ((bf16[8,128,768]{2,1,0:T(8,128)(2,1)}), bf16[8,128,768]{2,1,0:T(8,128)(2,1)S(1)}, u32[]{:S(2)}, u32[]{:S(2)}) async-start(bf16[8,128,768]{2,1,0:T(8,128)(2,1)} %bitcast.99), calls=%async_computation.2 | async-start | bytes 3145728 | tf_op jit(solution)/shard_map/all_to_all | solution.py:189
  244.5 363.9 %reduce-scatter.8.cloned.1.call-start = ((), (), s32[]{:S(2)}) async-start(), calls=%async_computation.11 | async-start | bytes 5898240 | tf_op jit(solution)/shard_map/reduce_scatter | solution.py:212
  313.9 40.6 %all-to-all-start.3 = ((bf16[8,128,768]{2,1,0:T(8,128)(2,1)}), bf16[8,128,768]{2,1,0:T(8,128)(2,1)S(1)}, u32[]{:S(2)}, u32[]{:S(2)}) async-start(bf16[8,128,768]{2,1,0:T(8,128)(2,1)} %bitcast.107), calls=%async_computation.3 | async-start | bytes 3145728 | tf_op jit(solution)/shard_map/all_to_all | solution.py:200
  317.5 293.8 %reduce-scatter.6.cloned.1.call-start = ((), (), s32[]{:S(2)}) async-start(), calls=%async_computation.10 | async-start | bytes 5898240 | tf_op jit(solution)/shard_map/reduce_scatter | solution.py:205
  354.5 40.9 %all-to-all-start.1 = ((bf16[8,128,768]{2,1,0:T(8,128)(2,1)}), bf16[8,128,768]{2,1,0:T(8,128)(2,1)}, u32[]{:S(2)}, u32[]{:S(2)}) async-start(bf16[8,128,768]{2,1,0:T(8,128)(2,1)} %bitcast.108), calls=%async_computation.1 | async-start | bytes 3145728 | tf_op jit(solution)/shard_map/all_to_all | solution.py:173
  358.8 281.2 %reduce-scatter.4.cloned.1.call-start = ((), (), s32[]{:S(2)}) async-start(), calls=%async_computation.9 | async-start | bytes 9732096 | tf_op jit(solution)/shard_map/reduce_scatter | solution.py:270
  441.5 35.1 %copy-start.5 = (f32[512,768]{1,0:T(8,128)S(1)}, f32[512,768]{1,0:T(8,128)}, u32[]{:S(2)}) copy-start(f32[512,768]{1,0:T(8,128)} %copy-done.4) | copy-start | bytes 4718596
  441.5 35.1 %copy-start.18 = (bf16[12,64,512]{2,1,0:T(8,128)(2,1)S(1)}, bf16[12,64,512]{2,1,0:T(8,128)(2,1)}, u32[]{:S(2)}) copy-start(bf16[12,64,512]{2,1,0:T(8,128)(2,1)} %copy-done.17) | copy-start | bytes 2359300
  441.5 37.3 %copy-start.10 = (bf16[512,768]{0,1:T(8,128)(2,1)S(1)}, bf16[512,768]{0,1:T(8,128)(2,1)}, u32[]{:S(2)}) copy-start(bf16[512,768]{0,1:T(8,128)(2,1)} %copy-done.9) | copy-start | bytes 2359300
  476.6 11.4 %slice-start.3 = ((s8[12582912]{0:T(1024)(128)(4,1)}), s8[4194304]{0:T(1024)(128)(4,1)S(1)}, s32[]{:S(2)}) async-start(s8[12582912]{0:T(1024)(128)(4,1)} %bitcast.86), calls=%async_computation.15 | async-start | bytes 8388608
  549.5 11.7 %copy-start.3 = (f32[512,768]{1,0:T(8,128)S(1)}, f32[512,768]{1,0:T(8,128)}, u32[]{:S(2)}) copy-start(f32[512,768]{1,0:T(8,128)} %copy-done.2) | copy-start | bytes 4718596
  549.5 12.8 %copy-start.20 = (bf16[12,64,512]{2,1,0:T(8,128)(2,1)S(1)}, bf16[12,64,512]{2,1,0:T(8,128)(2,1)}, u32[]{:S(2)}) copy-start(bf16[12,64,512]{2,1,0:T(8,128)(2,1)} %copy-done.19) | copy-start | bytes 2359300
  549.5 12.8 %copy-start.22 = (bf16[12,64,512]{2,1,0:T(8,128)(2,1)S(1)}, bf16[12,64,512]{2,1,0:T(8,128)(2,1)}, u32[]{:S(2)}) copy-start(bf16[12,64,512]{2,1,0:T(8,128)(2,1)} %copy-done.21) | copy-start | bytes 2359300
  549.5 12.8 %copy-start.29 = (bf16[768,2304]{1,0:T(8,128)(2,1)S(1)}, bf16[768,2304]{1,0:T(8,128)(2,1)}, u32[]{:S(2)}) copy-start(bf16[768,2304]{1,0:T(8,128)(2,1)} %all-gather.3.cloned.1.call-done) | copy-start | bytes 10616836
  (23 other events, 135.4 us)
Sparse Core Ops, SparseCore 0:
  9.6 33.4 all-gather.2
  44.6 17.4 all-gather.4
  291.4 46.8 reduce-scatter.7
  340.8 47.8 reduce-scatter.5
  505.2 134.7 reduce-scatter.3
where the time goes:
time: 658 us; the launch traced here: 650 us
  local copies, waits for them, and re-layouts  262 us (40%)
  waiting for transfers between devices  136 us (21%)
  matrix products  121 us (18%)
  other arithmetic  57.4 us (9%)
  blocking collectives  39.5 us (6%)
  starting transfers between devices  19.9 us (3%)
  between operations  14.8 us (2%)
    unnamed x81, local copies, waits for them, and re-layouts  113 us
    reshape x2, local copies, waits for them, and re-layouts, relative_bias(): tiled[:, :query_rows * (span_width - 1)]  76.8 us
    psum x1, blocking collectives, local(): lax.psum((table_grad, norm_gain_grad, ffn_gain_grad, router_grad), ('expe...  39.5 us
    all_to_all x1, waiting for transfers between devices, local(): lax.all_to_all(dispatched, 'expert', split_axis=0, concat_axis=0, tiled=T...  33.4 us
    all_to_all x1, waiting for transfers between devices, local(): lax.all_to_all(outgoing, 'expert', split_axis=0, concat_axis=0, tiled=True)  31.4 us
    dot_general x4, matrix products, contract_rows(): lax.dot_general(left_side, right_side, (((0,), (0,)), ((), ())), preferre...  26.2 us
    reduce_scatter x1, waiting for transfers between devices, local(): lax.psum_scatter(jnp.concatenate([contract_rows(normed_low, packed_grad),...  25.8 us
    all_to_all x1, waiting for transfers between devices, local(): lax.all_to_all(grad_buffer, 'expert', split_axis=0, concat_axis=0, tiled=...  25.7 us
  transfers between devices with their start and end apart: 9, of which 5 were waited for; matrix products, arithmetic and copies ran while one was open for 64% of the time, Pallas kernels for 0%

commit v1 on v0

v1 whole, which is shorter than its diff:
```python
import math

import jax
import jax.numpy as jnp
from jax import lax
from jax.experimental import pallas as pl
from jax.experimental.pallas import tpu as pltpu
from jax.sharding import PartitionSpec as P

MAXDIST = 128
TILE = 128


epsilon = 1e-06
neg_large = -1e30
highest = lax.Precision.HIGHEST


def thresholds(buckets, farthest):
    exact_count = buckets // 4
    return [
        math.ceil(exact_count * (farthest / exact_count) ** (tier_index / exact_count))
        for tier_index in range(1, exact_count)
    ]


def bucket_of(distance, buckets, farthest):
    exact_count = buckets // 4
    magnitude = jnp.abs(distance)
    beyond = exact_count + sum(
        (
            (magnitude >= edge_value).astype(jnp.int32)
            for edge_value in thresholds(buckets, farthest)
        )
    )
    near_far = jnp.where(magnitude < exact_count, magnitude, beyond)
    return jnp.where(distance > 0, 2 * exact_count, 0) + near_far


def bias_buckets(buckets):
    distance = jnp.arange(4 * TILE, dtype=jnp.int32) - 2 * TILE
    return (
        bucket_of(distance, buckets, MAXDIST)[:, None]
        == jnp.arange(buckets, dtype=jnp.int32)[None, :]
    ).astype(jnp.float32)


def skew(line):
    span = line.shape[1]
    rows = lax.broadcasted_iota(jnp.int32, (8, span), 0)
    tile = jnp.broadcast_to(line, (8, span))
    for step in (1, 2, 4):
        tile = jnp.where((rows & step) != 0, pltpu.roll(tile, step, 1), tile)
    step = 8
    while step < TILE:
        tile = jnp.concatenate([tile, pltpu.roll(tile, step, 1)], axis=0)
        step *= 2
    return tile


def skew_sum(tile):
    span = tile.shape[1]
    step = TILE // 2
    while step >= 8:
        tile = tile[:step] + pltpu.roll(tile[step:], span - step, 1)
        step //= 2
    for step in (4, 2, 1):
        tile = tile + pltpu.roll(pltpu.roll(tile, span - step, 1), 8 - step, 0)
    return tile[:1]


def tile_bias(strips, along, row_tile, tiles):
    pieces = []
    for column_tile in range(tiles):
        apart = column_tile - row_tile
        if abs(apart) <= 1:
            pieces.append(strips[:, (apart + 2) * TILE : (apart + 3) * TILE])
        else:
            edge = along[:, :TILE] if apart < 0 else along[:, 3 * TILE :]
            pieces.append(jnp.broadcast_to(edge, (TILE, TILE)))
    return jnp.concatenate(pieces, axis=1)


def half_masks(width, value):
    lanes = lax.broadcasted_iota(jnp.int32, (1, width), 1)
    first = jnp.where(lanes < width // 2, value, 0.0)
    return first.astype(jnp.bfloat16), (value - first).astype(jnp.bfloat16)


def two_heads(rows, masks):
    return jnp.concatenate([rows * masks[0], rows * masks[1]], axis=0)


def dot_last(left_side, right_side):
    return lax.dot_general(
        left_side, right_side, (((1,), (1,)), ((), ())), preferred_element_type=jnp.float32
    )


def dot_plain(left_side, right_side):
    return lax.dot_general(
        left_side, right_side, (((1,), (0,)), ((), ())), preferred_element_type=jnp.float32
    )


def pair_scores(queries, keys, strips, along, seg_col, seg_row, row_tile):
    tiles = keys.shape[0] // TILE
    bias = jnp.concatenate(
        [tile_bias(strips[head], along[head], row_tile, tiles) for head in range(2)], axis=0
    )
    rows = slice(row_tile * TILE, (row_tile + 1) * TILE)
    allowed = seg_col[rows] == seg_row
    allowed = jnp.concatenate([allowed, allowed], axis=0)
    return jnp.where(allowed, dot_last(queries, keys) + bias, neg_large)


def attend_kernel(q_ref, k_ref, v_ref, seg_col_ref, seg_row_ref, along_ref, out_ref, lse_ref):
    token_rows, pair = k_ref.shape
    keys, values = k_ref[...], v_ref[...]
    seg_col, seg_row = seg_col_ref[...], seg_row_ref[...]
    along = [along_ref[0, head : head + 1, :] for head in range(2)]
    strips = [skew(line) for line in along]
    masks = half_masks(pair, 0.125)
    first = lax.broadcasted_iota(jnp.int32, (TILE, pair), 1) < pair // 2
    for row_tile in range(token_rows // TILE):
        rows = slice(row_tile * TILE, (row_tile + 1) * TILE)
        queries = two_heads(q_ref[rows, :], masks)
        scores = pair_scores(queries, keys, strips, along, seg_col, seg_row, row_tile)
        largest = jnp.max(scores, axis=-1, keepdims=True)
        exp_scores = jnp.exp(scores - largest)
        totals = jnp.sum(exp_scores, axis=-1, keepdims=True)
        weights_low = (exp_scores * (1.0 / totals)).astype(jnp.bfloat16)
        mixed = dot_plain(weights_low, values)
        out_ref[rows, :] = jnp.where(first, mixed[:TILE], mixed[TILE:]).astype(jnp.bfloat16)
        log_totals = jnp.broadcast_to(largest + jnp.log(totals), (2 * TILE, pair))
        lse_ref[rows, :] = jnp.where(first, log_totals[:TILE], log_totals[TILE:])


def attend_back_kernel(
    q_ref,
    k_ref,
    v_ref,
    seg_col_ref,
    seg_row_ref,
    along_ref,
    lse_ref,
    grad_ref,
    q_grad_ref,
    k_grad_ref,
    v_grad_ref,
    along_grad_ref,
):
    token_rows, pair = k_ref.shape
    tiles = token_rows // TILE
    keys, values = k_ref[...], v_ref[...]
    seg_col, seg_row = seg_col_ref[...], seg_row_ref[...]
    along = [along_ref[0, head : head + 1, :] for head in range(2)]
    strips = [skew(line) for line in along]
    scaled = half_masks(pair, 0.125)
    ones = half_masks(pair, 1.0)
    keys_two = two_heads(keys, scaled)
    key_total = value_total = None
    sums = {}
    for row_tile in range(tiles):
        rows = slice(row_tile * TILE, (row_tile + 1) * TILE)
        queries = two_heads(q_ref[rows, :], scaled)
        upstream = two_heads(grad_ref[rows, :], ones)
        lse_both = lse_ref[rows, :]
        log_totals = jnp.concatenate(
            [lse_both[:, :1], lse_both[:, pair // 2 : pair // 2 + 1]], axis=0
        )
        scores = pair_scores(queries, keys, strips, along, seg_col, seg_row, row_tile)
        weights_soft = jnp.exp(scores - log_totals)
        prob_grad = dot_last(upstream, values)
        weighted = weights_soft * prob_grad
        centre = jnp.sum(weighted, axis=-1, keepdims=True)
        score_grad = (weighted - weights_soft * centre).astype(jnp.bfloat16)
        weights_low = weights_soft.astype(jnp.bfloat16)
        wide = jnp.concatenate([score_grad[:TILE], score_grad[TILE:]], axis=1)
        q_grad_ref[rows, :] = dot_plain(wide, keys_two).astype(jnp.bfloat16)
        key_part = contract_rows(score_grad, queries)
        value_part = contract_rows(weights_low, upstream)
        key_total = key_part if key_total is None else key_total + key_part
        value_total = value_part if value_total is None else value_total + value_part
        score_wide = score_grad.astype(jnp.float32)
        for head in range(2):
            for column_tile in range(tiles):
                apart = max(-2, min(2, column_tile - row_tile))
                piece = score_wide[
                    head * TILE : (head + 1) * TILE,
                    column_tile * TILE : (column_tile + 1) * TILE,
                ]
                had = sums.get((head, apart))
                sums[(head, apart)] = piece if had is None else had + piece
    k_grad_ref[...] = key_total.astype(jnp.bfloat16)
    v_grad_ref[...] = value_total.astype(jnp.bfloat16)
    zero = jnp.zeros((TILE, TILE), jnp.float32)
    for head in range(2):
        strip = jnp.concatenate(
            [zero] + [sums.get((head, apart), zero) for apart in (-1, 0, 1)], axis=1
        )
        nothing = jnp.zeros((1, TILE), jnp.float32)
        below, above = (
            jnp.sum(sums.get((head, apart), zero), axis=0, keepdims=True) for apart in (-2, 2)
        )
        far = jnp.concatenate([below, nothing, nothing, above], axis=1)
        along_grad_ref[0, head : head + 1, :] = skew_sum(strip) + far


def attention_specs(token_rows, pair, pairs):
    def part(which):
        return pl.BlockSpec((token_rows, pair), lambda step: (0, which * pairs + step))

    return [
        part(0),
        part(1),
        part(2),
        pl.BlockSpec((token_rows, 1), lambda step: (0, 0)),
        pl.BlockSpec((1, token_rows), lambda step: (0, 0)),
        pl.BlockSpec((1, 2, 4 * TILE), lambda step: (step, 0, 0)),
    ]


def attend(packed, segment_ids, along):
    token_rows, width = packed.shape[0], packed.shape[1] // 3
    pairs = along.shape[0]
    pair = width // pairs
    column = pl.BlockSpec((token_rows, pair), lambda step: (0, step))
    return pl.pallas_call(
        attend_kernel,
        grid=(pairs,),
        in_specs=attention_specs(token_rows, pair, pairs),
        out_specs=[column, column],
        out_shape=[
            jax.ShapeDtypeStruct((token_rows, width), jnp.bfloat16),
            jax.ShapeDtypeStruct((token_rows, width), jnp.float32),
        ],
        compiler_params=pltpu.CompilerParams(vmem_limit_bytes=40 * 1024 * 1024),
        cost_estimate=pl.CostEstimate(
            flops=4 * token_rows * token_rows * width,
            bytes_accessed=12 * token_rows * width,
            transcendentals=2 * pairs * token_rows * token_rows,
        ),
        name="attend",
    )(packed, packed, packed, segment_ids[:, None], segment_ids[None, :], along)


def attend_back(packed, segment_ids, along, log_totals, attended_grad):
    token_rows, width = packed.shape[0], packed.shape[1] // 3
    pairs = along.shape[0]
    pair = width // pairs
    column = pl.BlockSpec((token_rows, pair), lambda step: (0, step))
    line = pl.BlockSpec((1, 2, 4 * TILE), lambda step: (step, 0, 0))
    return pl.pallas_call(
        attend_back_kernel,
        grid=(pairs,),
        in_specs=attention_specs(token_rows, pair, pairs) + [column, column],
        out_specs=[column, column, column, line],
        out_shape=[jax.ShapeDtypeStruct((token_rows, width), jnp.bfloat16)] * 3
        + [jax.ShapeDtypeStruct(along.shape, jnp.float32)],
        compiler_params=pltpu.CompilerParams(vmem_limit_bytes=40 * 1024 * 1024),
        cost_estimate=pl.CostEstimate(
            flops=10 * token_rows * token_rows * width,
            bytes_accessed=18 * token_rows * width,
            transcendentals=2 * pairs * token_rows * token_rows,
        ),
        name="attend_back",
    )(
        packed,
        packed,
        packed,
        segment_ids[:, None],
        segment_ids[None, :],
        along,
        log_totals,
        attended_grad,
    )


def normalize(values, gain):
    scale_inv = lax.rsqrt(jnp.mean(values * values, axis=-1, keepdims=True) + epsilon)
    return (values * scale_inv * gain, scale_inv)


def norm_backward(values, scale_inv, gain, upstream):
    scaled = upstream * gain
    inner_mean = jnp.mean(scaled * values, axis=-1, keepdims=True)
    grad_values = scale_inv * scaled - values * scale_inv * scale_inv * scale_inv * inner_mean
    grad_gain = jnp.sum(upstream * values * scale_inv, axis=0)
    return (grad_values, grad_gain)


def gelu_value(values):
    return 0.5 * values * (1.0 + lax.erf(values * 0.7071067811865476))


def gelu_slope(values):
    return (
        0.5 * (1.0 + lax.erf(values * 0.7071067811865476))
        + values * jnp.exp(-0.5 * values * values) * 0.3989422804014327
    )


def contract_rows(left_side, right_side):
    return lax.dot_general(
        left_side, right_side, (((0,), (0,)), ((), ())), preferred_element_type=jnp.float32
    )


def local(
    tokens,
    segment_ids,
    routes,
    slots,
    qkv_weight,
    out_weight,
    bias_table,
    norm_gain,
    ffn_gain,
    router_weight,
    expert_in,
    expert_out,
    cotangent,
):
    token_rows, width = tokens.shape
    heads_count = bias_table.shape[1]
    experts_count = router_weight.shape[1]
    capacity = 2 * token_rows // experts_count
    weight_in = expert_in[0]
    weight_out = expert_out[0]
    full_qkv, full_out = (
        lax.all_gather(qkv_weight, "shard", axis=0, tiled=True),
        lax.all_gather(out_weight, "shard", axis=0, tiled=True),
    )
    inputs = tokens.astype(jnp.float32)
    normed, scale_one = normalize(inputs, norm_gain)
    normed_low = normed.astype(jnp.bfloat16)
    packed = jnp.dot(normed_low, full_qkv, preferred_element_type=jnp.float32).astype(jnp.bfloat16)
    buckets_hot = bias_buckets(bias_table.shape[0])
    along = jnp.dot(buckets_hot, bias_table, precision=highest).T.reshape(
        heads_count // 2, 2, 4 * TILE
    )
    mixed_blocks, log_totals = attend(packed, segment_ids, along)
    branch = jnp.dot(mixed_blocks, full_out, preferred_element_type=jnp.float32)
    middle = inputs + branch
    normed_two, scale_two = normalize(middle, ffn_gain)
    logits = jnp.dot(normed_two, router_weight, precision=highest)
    router_probs = jax.nn.softmax(logits, axis=-1)
    chosen = (routes[:, None] == jnp.arange(experts_count, dtype=jnp.int32)[None, :]).astype(
        jnp.float32
    )
    gates = jnp.sum(router_probs * chosen, axis=-1)
    sent = normed_two.astype(jnp.bfloat16)
    dest_rows = routes * capacity + slots
    outgoing = (
        jnp.zeros((experts_count * capacity, width), jnp.bfloat16)
        .at[dest_rows]
        .set(sent)
        .reshape(experts_count, capacity, width)
    )
    arrived_rows = lax.all_to_all(outgoing, "expert", split_axis=0, concat_axis=0, tiled=True)
    upstream = cotangent.astype(jnp.float32)
    row_grad = (gates[:, None] * upstream).astype(jnp.bfloat16)
    grad_buffer = (
        jnp.zeros((experts_count * capacity, width), jnp.bfloat16)
        .at[dest_rows]
        .set(row_grad)
        .reshape(experts_count, capacity, width)
    )
    grad_arrived = lax.all_to_all(grad_buffer, "expert", split_axis=0, concat_axis=0, tiled=True)
    flat_in = arrived_rows.reshape(-1, width)
    inner_flat = jnp.dot(flat_in, weight_in, preferred_element_type=jnp.float32)
    activated = gelu_value(inner_flat).astype(jnp.bfloat16)
    result_rows = jnp.dot(activated, weight_out, preferred_element_type=jnp.float32).astype(
        jnp.bfloat16
    )
    result_rows, flat_grad = lax.optimization_barrier(
        (result_rows, grad_arrived.reshape(-1, width))
    )
    coming_back = lax.all_to_all(
        result_rows.reshape(arrived_rows.shape), "expert", split_axis=0, concat_axis=0, tiled=True
    ).reshape(experts_count * capacity, width)
    act_grad = jnp.dot(flat_grad, weight_out.T, preferred_element_type=jnp.float32)
    inner_grad = (act_grad * gelu_slope(inner_flat)).astype(jnp.bfloat16)
    input_grad = jnp.dot(inner_grad, weight_in.T, preferred_element_type=jnp.float32).astype(
        jnp.bfloat16
    )
    input_grad, inner_grad, activated, flat_in, flat_grad = lax.optimization_barrier(
        (input_grad, inner_grad, activated, flat_in, flat_grad)
    )
    returned_grad = lax.all_to_all(
        input_grad.reshape(arrived_rows.shape), "expert", split_axis=0, concat_axis=0, tiled=True
    ).reshape(experts_count * capacity, width)
    expert_rows = jnp.take(coming_back, dest_rows, axis=0).astype(jnp.float32)
    layer_out = middle + gates[:, None] * expert_rows
    gate_grad = jnp.sum(upstream * expert_rows, axis=-1)
    sent_grad = jnp.take(returned_grad, dest_rows, axis=0).astype(jnp.float32)
    columns = flat_in
    grad_in_rows = lax.psum_scatter(
        contract_rows(columns, inner_grad).astype(jnp.bfloat16),
        "shard",
        scatter_dimension=0,
        tiled=True,
    ).astype(jnp.float32)
    columns = activated
    grad_out_rows = lax.psum_scatter(
        contract_rows(columns, flat_grad).astype(jnp.bfloat16),
        "shard",
        scatter_dimension=0,
        tiled=True,
    ).astype(jnp.float32)
    logit_grad = (gate_grad * gates)[:, None] * (chosen - router_probs)
    router_grad = lax.dot_general(
        normed_two, logit_grad, (((0,), (0,)), ((), ())), precision=highest
    )
    normed_two_grad = jnp.dot(logit_grad, router_weight.T, precision=highest) + sent_grad
    middle_norm_grad, ffn_gain_grad = norm_backward(middle, scale_two, ffn_gain, normed_two_grad)
    middle_grad = upstream + middle_norm_grad
    branch_grad = middle_grad.astype(jnp.bfloat16)
    attended_grad = jnp.dot(branch_grad, full_out.T, preferred_element_type=jnp.float32).astype(
        jnp.bfloat16
    )
    query_grads, key_grad, value_grad, along_grad = attend_back(
        packed, segment_ids, along, log_totals, attended_grad
    )
    table_grad = lax.dot_general(
        buckets_hot,
        along_grad.reshape(heads_count, 4 * TILE),
        (((0,), (1,)), ((), ())),
        precision=highest,
    )
    packed_grad = jnp.concatenate([query_grads, key_grad, value_grad], axis=1)
    normed_grad = jnp.dot(packed_grad, full_qkv.T, preferred_element_type=jnp.float32)
    input_norm_grad, norm_gain_grad = norm_backward(inputs, scale_one, norm_gain, normed_grad)
    grad_tokens = middle_grad + input_norm_grad
    grad_qkv = lax.psum_scatter(
        contract_rows(normed_low, packed_grad).astype(jnp.bfloat16),
        ("expert", "shard"),
        scatter_dimension=0,
        tiled=True,
    ).astype(jnp.float32)
    grad_out_weight = lax.psum_scatter(
        contract_rows(mixed_blocks, branch_grad).astype(jnp.bfloat16),
        ("expert", "shard"),
        scatter_dimension=0,
        tiled=True,
    ).astype(jnp.float32)
    table_grad, norm_gain_grad, ffn_gain_grad, router_grad = lax.psum(
        (table_grad, norm_gain_grad, ffn_gain_grad, router_grad), ("expert", "shard")
    )
    return (
        layer_out,
        grad_tokens,
        grad_qkv,
        grad_out_weight,
        table_grad,
        norm_gain_grad,
        ffn_gain_grad,
        router_grad,
        grad_in_rows[None],
        grad_out_rows[None],
    )


def solution(mesh):
    placed = (
        P(("expert", "shard"), None),
        P(("expert", "shard")),
        P(("expert", "shard")),
        P(("expert", "shard")),
        P("shard", None),
        P("shard", None),
        P(),
        P(),
        P(),
        P(),
        P("expert", None, None),
        P("expert", None, None),
        P(("expert", "shard"), None),
    )
    return jax.shard_map(
        local,
        mesh=mesh,
        in_specs=placed,
        out_specs=(
            P(("expert", "shard"), None),
            P(("expert", "shard"), None),
            P(("expert", "shard"), None),
            P(("expert", "shard"), None),
            P(),
            P(),
            P(),
            P(),
            P("expert", "shard", None),
            P("expert", "shard", None),
        ),
        check_vma=False,
    )
```

time: 658 us -> 571 us (0.87)
  local copies, waits for them, and re-layouts: 262 us -> 20.5 us
  waiting for transfers between devices: 136 us -> 321 us
  Pallas kernels: 0 us -> 34.3 us
  matrix products: 121 us -> 88.6 us
  other arithmetic: 57.4 us -> 25.2 us
    unnamed x81 -> x40, local copies, waits for them, and re-layouts: 113 us -> 10.2 us
    reduce_scatter x1 -> x2, waiting for transfers between devices: 25.8 us -> 103 us  [the longest x1 103 us: local(): lax.psum_scatter(contract_rows(normed_low, packed_grad).astype(jnp.bfloat...]
    reshape x2, local copies, waits for them, and re-layouts: 76.8 us -> 0.05 us  [the longest x1 0.03 us: local(): jnp.dot(buckets_hot, bias_table, precision=highest)]
    reduce_scatter x1, waiting for transfers between devices: 0.01 us -> 47.6 us  [local(): lax.psum_scatter(contract_rows(columns, flat_grad).astype(jnp.bfloat16),...]
    reduce_scatter x1, waiting for transfers between devices: 0.01 us -> 47.6 us  [local(): lax.psum_scatter(contract_rows(columns, inner_grad).astype(jnp.bfloat16),...]
    slice x8 -> x0, local copies, waits for them, and re-layouts: 40.1 us -> none  [the longest x1 22.6 us: relative_bias(): tiled[:, :query_rows * (span_width - 1)]]
    dot_general x10 -> x4, matrix products: 55.2 us -> 20.3 us  [the longest x1 10.6 us: local(): inner_flat = jnp.dot(flat_in, weight_in, preferred_element_type=jnp.float32)]
    pallas_call x0 -> x2, Pallas kernels: none -> 34.3 us  [the longest x1 20.4 us: attend_back(): pl.pallas_call(attend_back_kernel, grid=(pairs,), in_specs=attention_spec...]
  transfers between devices with their start and end apart: 9 -> 10, of which waited for: 5 -> 8; matrix products, arithmetic and copies ran while one was open for 64% -> 18% of each run, Pallas kernels for 0% -> 6%
where the time goes in v1:
time: 571 us; the launch traced here: 562 us
  waiting for transfers between devices  321 us (56%)
  matrix products  88.6 us (16%)
  blocking collectives  38.1 us (7%)
  Pallas kernels  34.3 us (6%)
  other arithmetic  25.2 us (4%)
  local copies, waits for them, and re-layouts  20.5 us (4%)
  starting transfers between devices  19.3 us (3%)
  between operations  14.9 us (3%)
    reduce_scatter x1, waiting for transfers between devices, local(): lax.psum_scatter(contract_rows(normed_low, packed_grad).astype(jnp.bfloat...  103 us
    reduce_scatter x1, waiting for transfers between devices, local(): lax.psum_scatter(contract_rows(columns, flat_grad).astype(jnp.bfloat16),...  47.6 us
    reduce_scatter x1, waiting for transfers between devices, local(): lax.psum_scatter(contract_rows(columns, inner_grad).astype(jnp.bfloat16),...  47.6 us
    psum x1, blocking collectives, local(): lax.psum((table_grad, norm_gain_grad, ffn_gain_grad, router_grad), ('expe...  38.1 us
    all_gather x1, waiting for transfers between devices, local(): lax.all_gather(qkv_weight, 'shard', axis=0, tiled=True)  32.2 us
    all_to_all x1, waiting for transfers between devices, local(): lax.all_to_all(outgoing, 'expert', split_axis=0, concat_axis=0, tiled=True)  29.9 us
    all_to_all x1, waiting for transfers between devices, local(): lax.all_to_all(input_grad.reshape(arrived_rows.shape), 'expert', split_ax...  29.8 us
    dot_general x4, matrix products, contract_rows(): lax.dot_general(left_side, right_side, (((0,), (0,)), ((), ())), preferre...  24.3 us
  transfers between devices with their start and end apart: 10, of which 8 were waited for; matrix products, arithmetic and copies ran while one was open for 18% of the time, Pallas kernels for 6%

profile of v1, /device:TPU:0, one launch (start us, length us, event | category | flops | bytes accessed | tf_op | source)
XLA Modules:
  0.0 561.7 jit_solution(12223293135221417113)
XLA Ops:
  10.9 32.2 %all-gather.3.cloned.1.call-done = bf16[768,2304]{1,0:T(8,128)(2,1)} async-done(((bf16[192,2304]{1,0:T(8,128)(2,1)}), bf16[768,2304]{1,0:T(8,128)(2,1)}) %all-gather.3.cloned.1.call-update) | async-done | bytes 3538960 | tf_op jit(solution)/shard_map/all_gather | solution.py:332
  47.2 13.8 %attend.1 = (bf16[512,768]{1,0:T(8,128)(2,1)S(1)}, f32[512,768]{1,0:T(8,128)S(1)}) custom-call(bf16[512,2304]{1,0:T(8,128)(2,1)S(1)} %convolution_convert_fusion.3.q_ref.k_ref.v_ref, bf16[512,2304]{1,0:T(8,128)(2,1)S(1)} %convolution_convert_fusion.3.q_ref.k_ref.v_ref, bf16[512,2304]{1,0:T(8,128)(2,1)S(1)} %convolution_convert_fusion.3.q_ref.k_ref.v_ref, ...), custom_call_target="tpu_custom_call" | custom-call | flops 805306368 | bytes 4718592 | tf_op jit(solution)/shard_map/attend/pallas_call | solution.py:229
  65.7 4.7 scatter_custom_fusion
  70.5 5.5 all-to-all-start
  79.1 4.5 scatter_custom_fusion.1
  83.6 29.9 %all-to-all-done = bf16[8,128,768]{2,1,0:T(8,128)(2,1)} async-done(((bf16[8,128,768]{2,1,0:T(8,128)(2,1)}), bf16[8,128,768]{2,1,0:T(8,128)(2,1)}, u32[]{:S(2)}, u32[]{:S(2)}) %all-to-all-start) | async-done | bytes 1572896 | tf_op jit(solution)/shard_map/all_to_all | solution.py:361
  113.5 4.5 all-to-all-start.1
  118.0 10.6 %multiply_convert_fusion = (bf16[1024,3072]{1,0:T(8,128)(2,1)S(1)}, f32[1024,3072]{1,0:T(8,128)}) fusion(bf16[1024,768]{1,0:T(8,128)(2,1)} %bitcast.4, bf16[1,768,3072]{2,1,0:T(8,128)(2,1)} %param.25), kind=kOutput, calls=%fused_computation.11 | convolution fusion | flops 4847566848 | bytes 25165824 | tf_op jit(solution)/shard_map/dot_general | solution.py:372
  131.1 8.5 %fusion.18 = bf16[1024,768]{1,0:T(8,128)(2,1)} fusion(bf16[1024,3072]{1,0:T(8,128)(2,1)S(1)} %get-tuple-element.35, bf16[1,3072,768]{2,1,0:T(8,128)(2,1)} %param.26), kind=kOutput, calls=%fused_computation.36 | convolution fusion | flops 4832624640 | bytes 12582912 | tf_op jit(solution)/shard_map/dot_general | solution.py:374
  139.6 15.0 %all-to-all-done.1 = bf16[8,128,768]{2,1,0:T(8,128)(2,1)} async-done(((bf16[8,128,768]{2,1,0:T(8,128)(2,1)}), bf16[8,128,768]{2,1,0:T(8,128)(2,1)}, u32[]{:S(2)}, u32[]{:S(2)}) %all-to-all-start.1) | async-done | bytes 1572896 | tf_op jit(solution)/shard_map/all_to_all | solution.py:370
  158.9 11.3 %fusion.5 = bf16[1024,3072]{1,0:T(8,128)(2,1)S(1)} fusion(f32[1024,3072]{1,0:T(8,128)} %get-tuple-element.52, bf16[1024,768]{1,0:T(8,128)(2,1)} %bitcast.8, bf16[1,3072,768]{2,1,0:T(8,128)(2,1)} %param.26), kind=kOutput, calls=%fused_computation.10 | convolution fusion | flops 4863295488 | bytes 25165824 | tf_op jit(solution)/shard_map/dot_general | solution.py:383
  172.9 8.5 %fusion.15 = bf16[1024,768]{1,0:T(8,128)(2,1)} fusion(bf16[1024,3072]{1,0:T(8,128)(2,1)S(1)} %fusion.5, bf16[1,768,3072]{2,1,0:T(8,128)(2,1)} %param.25), kind=kOutput, calls=%fused_computation.35 | convolution fusion | flops 4832624640 | bytes 12582912 | tf_op jit(solution)/shard_map/dot_general | solution.py:385
  181.4 14.1 %all-to-all-done.2 = bf16[8,128,768]{2,1,0:T(8,128)(2,1)} async-done(((bf16[8,128,768]{2,1,0:T(8,128)(2,1)}), bf16[8,128,768]{2,1,0:T(8,128)(2,1)}, u32[]{:S(2)}, u32[]{:S(2)}) %all-to-all-start.2) | async-done | bytes 1572896 | tf_op jit(solution)/shard_map/all_to_all | solution.py:380
  200.1 4.7 gather_fusion
  206.7 29.8 %all-to-all-done.3 = bf16[8,128,768]{2,1,0:T(8,128)(2,1)} async-done(((bf16[8,128,768]{2,1,0:T(8,128)(2,1)}), bf16[8,128,768]{2,1,0:T(8,128)(2,1)}, u32[]{:S(2)}, u32[]{:S(2)}) %all-to-all-start.3) | async-done | bytes 1572896 | tf_op jit(solution)/shard_map/all_to_all | solution.py:391
  236.5 4.7 gather_fusion.1
  252.6 20.4 %attend_back.1 = (bf16[512,768]{1,0:T(8,128)(2,1)S(1)}, bf16[512,768]{1,0:T(8,128)(2,1)S(1)}, bf16[512,768]{1,0:T(8,128)(2,1)S(1)}, f32[6,2,512]{2,1,0:T(2,128)S(1)}) custom-call(bf16[512,2304]{1,0:T(8,128)(2,1)S(1)} %convolution_convert_fusion.3.q_ref.k_ref.v_ref, bf16[512,2304]{1,0:T(8,128)(2,1)S(1)} %convolution_convert_fusion.3.q_ref.k_ref.v_ref, ...), custom_call_target="tpu_custom_call" | custom-call | flops 2013265920 | bytes 7077888 | tf_op jit(solution)/shard_map/attend_back/pallas_call | solution.py:254
  279.0 9.3 %convolution_convert_fusion = bf16[3072,768]{1,0:T(8,128)(2,1)} fusion(bf16[1024,3072]{1,0:T(8,128)(2,1)} %copy-done.18, bf16[1024,768]{1,0:T(8,128)(2,1)} %bitcast.8), kind=kOutput, calls=%fused_computation.13 | convolution fusion | flops 4834197504 | bytes 12582912 | tf_op jit(solution)/shard_map/dot_general | solution.py:305
  288.3 9.2 %convolution_convert_fusion.1 = bf16[768,3072]{1,0:T(8,128)(2,1)} fusion(bf16[1024,768]{1,0:T(8,128)(2,1)} %bitcast.4, bf16[1024,3072]{1,0:T(8,128)(2,1)} %copy-done.17), kind=kOutput, calls=%fused_computation.14 | convolution fusion | flops 4834197504 | bytes 12582912 | tf_op jit(solution)/shard_map/dot_general | solution.py:305
  300.0 6.2 %fusion.32 = (f32[768]{0:T(1024)S(1)}, f32[512]{0:T(512)S(1)}, f32[512,768]{1,0:T(8,128)}) fusion(bf16[512,768]{1,0:T(8,128)(2,1)S(1)} %copy-done.11, f32[512]{0:T(512)S(1)} %add_rsqrt_fusion.1, f32[768]{0:T(1024)S(1)} %copy-done.15, bf16[512,2304]{1,0:T(8,128)(2,1)} %copy-done.12, bf16[768,2304]{1,0:T(8,128)(2,1)} %all-gather.3.cloned.1.call-done), kind=kOutput, calls=%fused_computation.48 | convolution fusion | flops 1814690560 | bytes 8267776 | tf_op jit(solution)/shard_map/dot_general | solution.py:433
  306.2 38.1 %all-reduce = (f32[32,12]{0,1:T(8,128)}, f32[768]{0:T(1024)}, f32[768]{0:T(1024)}, f32[768,8]{0,1:T(8,128)}) all-reduce(f32[32,12]{0,1:T(8,128)S(1)} %fusion.51, f32[768]{0:T(1024)S(1)} %get-tuple-element.39, f32[768]{0:T(1024)S(1)} %get-tuple-element.37, ...), channel_id=1, replica_groups=mesh['expert'=8,'shard'=4] {'expert','shard'}, use_global_device_ids=true, to_apply=%region_12.14 | all-reduce | flops 8064 | bytes 64512 | tf_op jit(solution)/shard_map/psum | solution.py:448
  348.8 103.0 %reduce-scatter.5.cloned.1.call-done = bf16[24,2304]{1,0:T(8,128)(2,1)} async-done(((bf16[768,2304]{1,0:T(8,128)(2,1)}), bf16[24,2304]{1,0:T(8,128)(2,1)}) %reduce-scatter.5.cloned.1.call-update) | async-done | bytes 110608 | tf_op jit(solution)/shard_map/reduce_scatter | solution.py:436
  453.4 47.6 %reduce-scatter.11.cloned.1.call-done = bf16[768,768]{1,0:T(8,128)(2,1)} async-done(((bf16[3072,768]{1,0:T(8,128)(2,1)}), bf16[768,768]{1,0:T(8,128)(2,1)}) %reduce-scatter.11.cloned.1.call-update) | async-done | bytes 1179664 | tf_op jit(solution)/shard_map/reduce_scatter | solution.py:406
  503.9 47.6 %reduce-scatter.9.cloned.1.call-done = bf16[192,3072]{1,0:T(8,128)(2,1)} async-done(((bf16[768,3072]{1,0:T(8,128)(2,1)}), bf16[192,3072]{1,0:T(8,128)(2,1)}) %reduce-scatter.9.cloned.1.call-update) | async-done | bytes 1179664 | tf_op jit(solution)/shard_map/reduce_scatter | solution.py:399
  (88 shorter events, 63.1 us)
Async XLA Ops:
  7.2 68.8 %copy-start = (f32[768,8]{0,1:T(8,128)S(1)}, f32[768,8]{0,1:T(8,128)}, u32[]{:S(2)}) copy-start(f32[768,8]{0,1:T(8,128)} %param.24) | copy-start | bytes 73732
  7.2 3.4 copy-start.10
  7.2 3.7 copy-start.14
  7.2 3.7 copy-start.16
  7.2 35.9 %copy-start.15 = (f32[768]{0:T(1024)S(1)}, f32[768]{0:T(1024)}, u32[]{:S(2)}) copy-start(f32[768]{0:T(1024)} %param.22) | copy-start | bytes 9220
  7.2 35.9 %all-gather.3.cloned.1.call-start = ((), (), s32[]{:S(2)}) async-start(), calls=%async_computation.8 | async-start | bytes 4423680 | tf_op jit(solution)/shard_map/all_gather | solution.py:332
  8.0 54.3 %all-gather.5.cloned.1.call-start = ((), (), s32[]{:S(2)}) async-start(), calls=%async_computation.9 | async-start | bytes 1474560 | tf_op jit(solution)/shard_map/all_gather | solution.py:333
  10.9 36.3 %copy-start.3 = (s32[512]{0:T(512)S(1)}, s32[512]{0:T(512)}, u32[]{:S(2)}) copy-start(s32[512]{0:T(512)} %param.16) | copy-start | bytes 6148
  62.3 3.4 copy-start.13
  70.5 43.0 %all-to-all-start = ((bf16[8,128,768]{2,1,0:T(8,128)(2,1)}), bf16[8,128,768]{2,1,0:T(8,128)(2,1)}, u32[]{:S(2)}, u32[]{:S(2)}) async-start(bf16[8,128,768]{2,1,0:T(8,128)(2,1)} %bitcast.58), calls=%async_computation | async-start | bytes 3145728 | tf_op jit(solution)/shard_map/all_to_all | solution.py:361
  113.5 41.1 %all-to-all-start.1 = ((bf16[8,128,768]{2,1,0:T(8,128)(2,1)}), bf16[8,128,768]{2,1,0:T(8,128)(2,1)}, u32[]{:S(2)}, u32[]{:S(2)}) async-start(bf16[8,128,768]{2,1,0:T(8,128)(2,1)} %bitcast.57), calls=%async_computation.1 | async-start | bytes 3145728 | tf_op jit(solution)/shard_map/all_to_all | solution.py:370
  128.5 2.6 copy-start.18
  154.6 40.9 %all-to-all-start.2 = ((bf16[8,128,768]{2,1,0:T(8,128)(2,1)}), bf16[8,128,768]{2,1,0:T(8,128)(2,1)}, u32[]{:S(2)}, u32[]{:S(2)}) async-start(bf16[8,128,768]{2,1,0:T(8,128)(2,1)} %bitcast.60), calls=%async_computation.2 | async-start | bytes 3145728 | tf_op jit(solution)/shard_map/all_to_all | solution.py:380
  170.2 2.7 copy-start.17
  195.5 40.9 %all-to-all-start.3 = ((bf16[8,128,768]{2,1,0:T(8,128)(2,1)}), bf16[8,128,768]{2,1,0:T(8,128)(2,1)}, u32[]{:S(2)}, u32[]{:S(2)}) async-start(bf16[8,128,768]{2,1,0:T(8,128)(2,1)} %bitcast.59), calls=%async_computation.3 | async-start | bytes 3145728 | tf_op jit(solution)/shard_map/all_to_all | solution.py:391
  199.8 147.5 %reduce-scatter.7.cloned.1.call-start = ((), (), s32[]{:S(2)}) async-start(), calls=%async_computation.11 | async-start | bytes 1216512 | tf_op jit(solution)/shard_map/reduce_scatter | solution.py:442
  241.2 3.7 copy-start.4
  241.2 3.7 copy-start.8
  241.2 3.7 copy-start.9
  249.9 201.9 %reduce-scatter.5.cloned.1.call-start = ((), (), s32[]{:S(2)}) async-start(), calls=%async_computation.10 | async-start | bytes 3649536 | tf_op jit(solution)/shard_map/reduce_scatter | solution.py:436
  249.9 2.7 copy-start.2
  278.7 222.3 %reduce-scatter.11.cloned.1.call-start = ((), (), s32[]{:S(2)}) async-start(), calls=%async_computation.13 | async-start | bytes 5898240 | tf_op jit(solution)/shard_map/reduce_scatter | solution.py:406
  288.3 263.2 %reduce-scatter.9.cloned.1.call-start = ((), (), s32[]{:S(2)}) async-start(), calls=%async_computation.12 | async-start | bytes 5898240 | tf_op jit(solution)/shard_map/reduce_scatter | solution.py:399
  300.0 44.3 %copy-start.7 = (f32[512,768]{1,0:T(8,128)S(1)}, f32[512,768]{1,0:T(8,128)}, u32[]{:S(2)}) copy-start(f32[512,768]{1,0:T(8,128)} %copy-done.6) | copy-start | bytes 4718596
  (5 other events, 6.7 us)
Sparse Core Ops, SparseCore 0:
  9.6 33.4 all-gather.2
  44.7 17.5 all-gather.4
  250.0 94.3 reduce-scatter.6
  349.7 102.1 reduce-scatter.4
  454.2 46.7 reduce-scatter.10
  503.6 47.8 reduce-scatter.8

commit v2 on v1

--- a/solution.py
+++ b/solution.py
@@ -307,6 +307,63 @@
     )
 
 
+def swap(values, axes, count, bit):
+    return lax.ppermute(values, axes, [(rank, rank ^ bit) for rank in range(count)])
+
+
+def gather_rows(block):
+    count = lax.axis_size("shard")
+    rank = lax.axis_index("shard")
+    pieces = {0: block}
+    for apart in sorted(range(1, count), key=lambda apart: (apart & 1, -apart)):
+        if not apart & 1:
+            pieces[apart] = swap(block, "shard", count, apart)
+    for apart in range(1, count, 2):
+        pieces[apart] = swap(pieces[apart ^ 1], "shard", count, 1)
+    rows = block.shape[0]
+    full = jnp.zeros((count * rows,) + block.shape[1:], block.dtype)
+    for apart in range(count):
+        full = lax.dynamic_update_slice_in_dim(full, pieces[apart], (rank ^ apart) * rows, axis=0)
+    return full
+
+
+def scatter_sum(partial):
+    owners, count = lax.axis_size("expert"), lax.axis_size("shard")
+    rank = lax.axis_index("shard")
+    columns = partial.shape[1]
+    rows = partial.shape[0] // (owners * count)
+    held = partial.astype(jnp.bfloat16)
+    left, bit = count, 1
+    while bit < count:
+        held = held.reshape(owners, left // 2, 2, rows, columns)
+        side = (rank // bit) % 2
+        mine = lax.dynamic_index_in_dim(held, side, axis=2, keepdims=False)
+        other = lax.dynamic_index_in_dim(held, 1 - side, axis=2, keepdims=False)
+        came = swap(other, "shard", count, bit)
+        held = (mine.astype(jnp.float32) + came.astype(jnp.float32)).astype(jnp.bfloat16)
+        left //= 2
+        bit *= 2
+    held = held.reshape(owners, rows, columns)
+    held = lax.all_to_all(held, "expert", split_axis=0, concat_axis=0, tiled=True)
+    return jnp.sum(held.astype(jnp.float32), axis=0)
+
+
+def sum_everywhere(arrays):
+    axes = ("expert", "shard")
+    count = lax.axis_size("expert") * lax.axis_size("shard")
+    flat = jnp.concatenate([values.reshape(-1, 128) for values in arrays], axis=0)
+    bit = 1
+    while bit < count:
+        flat = flat + swap(flat, axes, count, bit)
+        bit *= 2
+    results, start = [], 0
+    for values in arrays:
+        rows = values.size // 128
+        results.append(flat[start : start + rows].reshape(values.shape))
+        start += rows
+    return results
+
+
 def local(
     tokens,
     segment_ids,
@@ -328,10 +385,7 @@
     capacity = 2 * token_rows // experts_count
     weight_in = expert_in[0]
     weight_out = expert_out[0]
-    full_qkv, full_out = (
-        lax.all_gather(qkv_weight, "shard", axis=0, tiled=True),
-        lax.all_gather(out_weight, "shard", axis=0, tiled=True),
-    )
+    full_qkv, full_out = gather_rows(qkv_weight), gather_rows(out_weight)
     inputs = tokens.astype(jnp.float32)
     normed, scale_one = normalize(inputs, norm_gain)
     normed_low = normed.astype(jnp.bfloat16)
@@ -385,30 +439,23 @@
     input_grad = jnp.dot(inner_grad, weight_in.T, preferred_element_type=jnp.float32).astype(
         jnp.bfloat16
     )
-    input_grad, inner_grad, activated, flat_in, flat_grad = lax.optimization_barrier(
-        (input_grad, inner_grad, activated, flat_in, flat_grad)
+    out_partial = contract_rows(activated, flat_grad).astype(jnp.bfloat16)
+    input_grad, inner_grad, flat_in, out_partial = lax.optimization_barrier(
+        (input_grad, inner_grad, flat_in, out_partial)
     )
     returned_grad = lax.all_to_all(
         input_grad.reshape(arrived_rows.shape), "expert", split_axis=0, concat_axis=0, tiled=True
     ).reshape(experts_count * capacity, width)
+    in_partial = contract_rows(flat_in, inner_grad).astype(jnp.bfloat16)
+    returned_grad, in_partial = lax.optimization_barrier((returned_grad, in_partial))
     expert_rows = jnp.take(coming_back, dest_rows, axis=0).astype(jnp.float32)
     layer_out = middle + gates[:, None] * expert_rows
     gate_grad = jnp.sum(upstream * expert_rows, axis=-1)
     sent_grad = jnp.take(returned_grad, dest_rows, axis=0).astype(jnp.float32)
-    columns = flat_in
-    grad_in_rows = lax.psum_scatter(
-        contract_rows(columns, inner_grad).astype(jnp.bfloat16),
-        "shard",
-        scatter_dimension=0,
-        tiled=True,
-    ).astype(jnp.float32)
-    columns = activated
-    grad_out_rows = lax.psum_scatter(
-        contract_rows(columns, flat_grad).astype(jnp.bfloat16),
-        "shard",
-        scatter_dimension=0,
-        tiled=True,
-    ).astype(jnp.float32)
+    grad_out_rows = lax.psum_scatter(out_partial, "shard", scatter_dimension=0, tiled=True)
+    grad_in_rows = lax.psum_scatter(in_partial, "shard", scatter_dimension=0, tiled=True).astype(
+        jnp.float32
+    )
     logit_grad = (gate_grad * gates)[:, None] * (chosen - router_probs)
     router_grad = lax.dot_general(
         normed_two, logit_grad, (((0,), (0,)), ((), ())), precision=highest
@@ -420,6 +467,8 @@
     attended_grad = jnp.dot(branch_grad, full_out.T, preferred_element_type=jnp.float32).astype(
         jnp.bfloat16
     )
+    attended_grad, grad_out_rows = lax.optimization_barrier((attended_grad, grad_out_rows))
+    grad_out_rows = grad_out_rows.astype(jnp.float32)
     query_grads, key_grad, value_grad, along_grad = attend_back(
         packed, segment_ids, along, log_totals, attended_grad
     )
@@ -433,20 +482,10 @@
     normed_grad = jnp.dot(packed_grad, full_qkv.T, preferred_element_type=jnp.float32)
     input_norm_grad, norm_gain_grad = norm_backward(inputs, scale_one, norm_gain, normed_grad)
     grad_tokens = middle_grad + input_norm_grad
-    grad_qkv = lax.psum_scatter(
-        contract_rows(normed_low, packed_grad).astype(jnp.bfloat16),
-        ("expert", "shard"),
-        scatter_dimension=0,
-        tiled=True,
-    ).astype(jnp.float32)
-    grad_out_weight = lax.psum_scatter(
-        contract_rows(mixed_blocks, branch_grad).astype(jnp.bfloat16),
-        ("expert", "shard"),
-        scatter_dimension=0,
-        tiled=True,
-    ).astype(jnp.float32)
-    table_grad, norm_gain_grad, ffn_gain_grad, router_grad = lax.psum(
-        (table_grad, norm_gain_grad, ffn_gain_grad, router_grad), ("expert", "shard")
+    grad_out_weight = scatter_sum(contract_rows(mixed_blocks, branch_grad))
+    grad_qkv = scatter_sum(contract_rows(normed_low, packed_grad))
+    table_grad, norm_gain_grad, ffn_gain_grad, router_grad = sum_everywhere(
+        (table_grad, norm_gain_grad, ffn_gain_grad, router_grad)
     )
     return (
         layer_out,

time: 571 us -> 419 us (0.73)
  waiting for transfers between devices: 321 us -> 130 us
  starting transfers between devices: 19.3 us -> 38.4 us
  local copies, waits for them, and re-layouts: 20.5 us -> 38.5 us
    reduce_scatter x4 -> x2, waiting for transfers between devices: 198 us -> 0.02 us  [the longest x1 0.02 us: local(): lax.psum_scatter(out_partial, 'shard', scatter_dimension=0, tiled=True)]
    ppermute x0 -> x15, waiting for transfers between devices: none -> 58.7 us  [swap(): lax.ppermute(values, axes, [(rank, rank ^ bit) for rank in range(count)])]
    all_to_all x0 -> x1, blocking collectives: none -> 41 us  [local(): lax.all_to_all(input_grad.reshape(arrived_rows.shape), 'expert', split_ax...]
    psum x1 -> x0, blocking collectives: 38.1 us -> none  [local(): lax.psum((table_grad, norm_gain_grad, ffn_gain_grad, router_grad), ('expe...]
    all_gather x2 -> x0, waiting for transfers between devices: 32.2 us -> none  [the longest x1 32.2 us: local(): lax.all_gather(qkv_weight, 'shard', axis=0, tiled=True)]
    all_to_all x1 -> x2, waiting for transfers between devices: 29.8 us -> 0.01 us  [scatter_sum(): lax.all_to_all(held, 'expert', split_axis=0, concat_axis=0, tiled=True)]
    ppermute x0 -> x15, starting transfers between devices: none -> 14.7 us  [swap(): lax.ppermute(values, axes, [(rank, rank ^ bit) for rank in range(count)])]
    all_to_all x1, waiting for transfers between devices: 14.1 us -> 26.6 us  [local(): lax.all_to_all(result_rows.reshape(arrived_rows.shape), 'expert', split_a...]
  transfers between devices with their start and end apart: 10 -> 22, of which waited for: 8 -> 9; matrix products, arithmetic and copies ran while one was open for 18% -> 25% of each run, Pallas kernels for 6% -> 5%
where the time goes in v2:
time: 419 us; the launch traced here: 412 us
  waiting for transfers between devices  130 us (31%)
  matrix products  84 us (20%)
  blocking collectives  41 us (10%)
  local copies, waits for them, and re-layouts  38.5 us (9%)
  starting transfers between devices  38.4 us (9%)
  Pallas kernels  34.5 us (8%)
  other arithmetic  30.3 us (7%)
  between operations  14.9 us (4%)
    ppermute x15, waiting for transfers between devices, swap(): lax.ppermute(values, axes, [(rank, rank ^ bit) for rank in range(count)])  58.7 us
    all_to_all x1, blocking collectives, local(): lax.all_to_all(input_grad.reshape(arrived_rows.shape), 'expert', split_ax...  41 us
    all_to_all x1, waiting for transfers between devices, local(): lax.all_to_all(outgoing, 'expert', split_axis=0, concat_axis=0, tiled=True)  29.6 us
    all_to_all x1, waiting for transfers between devices, local(): lax.all_to_all(result_rows.reshape(arrived_rows.shape), 'expert', split_a...  26.6 us
    dot_general x4, matrix products, contract_rows(): lax.dot_general(left_side, right_side, (((0,), (0,)), ((), ())), preferre...  21.4 us
    pallas_call x1, Pallas kernels, attend_back(): pl.pallas_call(attend_back_kernel, grid=(pairs,), in_specs=attention_spec...  20.6 us
    all_to_all x1, waiting for transfers between devices, local(): lax.all_to_all(grad_buffer, 'expert', split_axis=0, concat_axis=0, tiled=...  15.1 us
    ppermute x15, starting transfers between devices, swap(): lax.ppermute(values, axes, [(rank, rank ^ bit) for rank in range(count)])  14.7 us
  transfers between devices with their start and end apart: 22, of which 9 were waited for; matrix products, arithmetic and copies ran while one was open for 25% of the time, Pallas kernels for 5%

profile of v2, /device:TPU:0, one launch (start us, length us, event | category | flops | bytes accessed | tf_op | source)
XLA Modules:
  0.0 411.6 jit_solution(10536885725293624796)
XLA Ops:
  14.6 22.6 %collective-permute-done.4 = bf16[192,768]{1,0:T(8,128)(2,1)} collective-permute-done((bf16[192,768]{1,0:T(8,128)(2,1)}, bf16[192,768]{1,0:T(8,128)(2,1)}, u32[]{:S(2)}, u32[]{:S(2)}) %collective-permute-start.4) | collective-permute-done | bytes 294944 | tf_op jit(solution)/shard_map/ppermute | solution.py:311
  51.1 13.8 %attend.1 = (bf16[512,768]{1,0:T(8,128)(2,1)S(1)}, f32[512,768]{1,0:T(8,128)S(1)}) custom-call(bf16[512,2304]{1,0:T(8,128)(2,1)S(1)} %convolution_convert_fusion.3.q_ref.k_ref.v_ref, bf16[512,2304]{1,0:T(8,128)(2,1)S(1)} %convolution_convert_fusion.3.q_ref.k_ref.v_ref, bf16[512,2304]{1,0:T(8,128)(2,1)S(1)} %convolution_convert_fusion.3.q_ref.k_ref.v_ref, ...), custom_call_target="tpu_custom_call" | custom-call | flops 805306368 | bytes 4718592 | tf_op jit(solution)/shard_map/attend/pallas_call | solution.py:229
  66.9 4.7 %scatter_custom_fusion = bf16[1024,768]{1,0:T(8,128)(2,1)} fusion(s32[512]{0:T(512)S(1)} %get-tuple-element.58, f32[512,768]{1,0:T(8,128)} %get-tuple-element.64, bf16[]{:T(256)} %constant.119.clone.1, f32[768]{0:T(1024)S(1)} %copy-done.23, f32[512]{0:T(512)S(1)} %add_rsqrt_fusion), kind=kCustom, calls=%fused_computation.70 | custom fusion | flops 1179648 | bytes 3151874 | tf_op jit(solution)/shard_map/scatter | solution.py:412
  71.7 6.6 %all-to-all-start = ((bf16[8,128,768]{2,1,0:T(8,128)(2,1)}), bf16[8,128,768]{2,1,0:T(8,128)(2,1)}, u32[]{:S(2)}, u32[]{:S(2)}) async-start(bf16[8,128,768]{2,1,0:T(8,128)(2,1)} %bitcast.81), calls=%async_computation | async-start | bytes 3145728 | tf_op jit(solution)/shard_map/all_to_all | solution.py:415
  81.4 4.5 %scatter_custom_fusion.1 = bf16[1024,768]{1,0:T(8,128)(2,1)} fusion(s32[512]{0:T(512)S(1)} %get-tuple-element.58, bf16[512,768]{1,0:T(8,128)(2,1)} %param.27, bf16[]{:T(256)} %constant.119.clone.1, f32[512]{0:T(512)S(1)} %select_reduce_fusion), kind=kCustom, calls=%fused_computation.71 | custom fusion | flops 1179648 | bytes 2361346 | tf_op jit(solution)/shard_map/scatter | solution.py:421
  85.9 29.6 %all-to-all-done = bf16[8,128,768]{2,1,0:T(8,128)(2,1)} async-done(((bf16[8,128,768]{2,1,0:T(8,128)(2,1)}), bf16[8,128,768]{2,1,0:T(8,128)(2,1)}, u32[]{:S(2)}, u32[]{:S(2)}) %all-to-all-start) | async-done | bytes 1572896 | tf_op jit(solution)/shard_map/all_to_all | solution.py:415
  115.4 4.3 %all-to-all-start.1 = ((bf16[8,128,768]{2,1,0:T(8,128)(2,1)}), bf16[8,128,768]{2,1,0:T(8,128)(2,1)}, u32[]{:S(2)}, u32[]{:S(2)}) async-start(bf16[8,128,768]{2,1,0:T(8,128)(2,1)} %bitcast.80), calls=%async_computation.1 | async-start | bytes 3145728 | tf_op jit(solution)/shard_map/all_to_all | solution.py:424
  119.8 10.5 %multiply_convert_fusion = (bf16[1024,3072]{1,0:T(8,128)(2,1)S(1)}, f32[1024,3072]{1,0:T(8,128)}) fusion(bf16[1024,768]{1,0:T(8,128)(2,1)} %bitcast.4, bf16[1,768,3072]{2,1,0:T(8,128)(2,1)} %param.25), kind=kOutput, calls=%fused_computation.11 | convolution fusion | flops 4847566848 | bytes 25165824 | tf_op jit(solution)/shard_map/dot_general | solution.py:426
  132.8 8.4 %fusion.19 = bf16[1024,768]{1,0:T(8,128)(2,1)} fusion(bf16[1024,3072]{1,0:T(8,128)(2,1)S(1)} %get-tuple-element.65, bf16[1,3072,768]{2,1,0:T(8,128)(2,1)} %param.26), kind=kOutput, calls=%fused_computation.41 | convolution fusion | flops 4832624640 | bytes 12582912 | tf_op jit(solution)/shard_map/dot_general | solution.py:428
  141.3 15.1 %all-to-all-done.1 = bf16[8,128,768]{2,1,0:T(8,128)(2,1)} async-done(((bf16[8,128,768]{2,1,0:T(8,128)(2,1)}), bf16[8,128,768]{2,1,0:T(8,128)(2,1)}, u32[]{:S(2)}, u32[]{:S(2)}) %all-to-all-start.1) | async-done | bytes 1572896 | tf_op jit(solution)/shard_map/all_to_all | solution.py:424
  156.4 9.1 %convolution_convert_fusion.1 = bf16[3072,768]{1,0:T(8,128)(2,1)} fusion(bf16[1024,3072]{1,0:T(8,128)(2,1)} %copy-done.29, bf16[1024,768]{1,0:T(8,128)(2,1)} %bitcast.8), kind=kOutput, calls=%fused_computation.14 | convolution fusion | flops 4834197504 | bytes 12582912 | tf_op jit(solution)/shard_map/dot_general | solution.py:305
  165.5 11.3 %fusion.5 = bf16[1024,3072]{1,0:T(8,128)(2,1)S(1)} fusion(f32[1024,3072]{1,0:T(8,128)} %get-tuple-element.66, bf16[1024,768]{1,0:T(8,128)(2,1)} %bitcast.8, bf16[1,3072,768]{2,1,0:T(8,128)(2,1)} %param.26), kind=kOutput, calls=%fused_computation.10 | convolution fusion | flops 4863295488 | bytes 25165824 | tf_op jit(solution)/shard_map/dot_general | solution.py:437
  179.5 8.5 %fusion.16 = bf16[1024,768]{1,0:T(8,128)(2,1)} fusion(bf16[1024,3072]{1,0:T(8,128)(2,1)S(1)} %fusion.5, bf16[1,768,3072]{2,1,0:T(8,128)(2,1)} %param.25), kind=kOutput, calls=%fused_computation.40 | convolution fusion | flops 4832624640 | bytes 12582912 | tf_op jit(solution)/shard_map/dot_general | solution.py:439
  188.0 41.0 %all_to_all.30 = bf16[8,128,768]{2,1,0:T(8,128)(2,1)} all-to-all(bf16[8,128,768]{2,1,0:T(8,128)(2,1)} %bitcast.87), channel_id=1, replica_groups=mesh['expert'=8,'shard'=4] {'expert'}, dimensions={0} | all-to-all | bytes 3145728 | tf_op jit(solution)/shard_map/all_to_all | solution.py:446
  229.0 4.3 %all-to-all-start.2 = ((bf16[8,128,768]{2,1,0:T(8,128)(2,1)}), bf16[8,128,768]{2,1,0:T(8,128)(2,1)}, u32[]{:S(2)}, u32[]{:S(2)}) async-start(bf16[8,128,768]{2,1,0:T(8,128)(2,1)} %bitcast.86), calls=%async_computation.2 | async-start | bytes 3145728 | tf_op jit(solution)/shard_map/all_to_all | solution.py:434
  233.5 9.3 %convolution_convert_fusion = bf16[768,3072]{1,0:T(8,128)(2,1)} fusion(bf16[1024,768]{1,0:T(8,128)(2,1)} %bitcast.4, bf16[1024,3072]{1,0:T(8,128)(2,1)} %copy-done.28), kind=kOutput, calls=%fused_computation.13 | convolution fusion | flops 4834197504 | bytes 12582912 | tf_op jit(solution)/shard_map/dot_general | solution.py:305
  242.9 26.6 %all-to-all-done.2 = bf16[8,128,768]{2,1,0:T(8,128)(2,1)} async-done(((bf16[8,128,768]{2,1,0:T(8,128)(2,1)}), bf16[8,128,768]{2,1,0:T(8,128)(2,1)}, u32[]{:S(2)}, u32[]{:S(2)}) %all-to-all-start.2) | async-done | bytes 1572896 | tf_op jit(solution)/shard_map/all_to_all | solution.py:434
  269.5 4.7 %gather_fusion = bf16[512,768]{1,0:T(8,128)(2,1)} fusion(bf16[1024,768]{1,0:T(8,128)(2,1)} %bitcast.10, s32[1024]{0:T(1024)S(1)} %pad_clamp_fusion), kind=kCustom, calls=%fused_computation.clone | custom fusion | bytes 1574912 | tf_op jit(solution)/shard_map/jit(_take)/gather | solution.py:451
  276.0 4.7 %gather_fusion.1 = bf16[512,768]{1,0:T(8,128)(2,1)} fusion(bf16[1024,768]{1,0:T(8,128)(2,1)} %bitcast.79, s32[1024]{0:T(1024)S(1)} %pad_clamp_fusion), kind=kCustom, calls=%fused_computation.1.clone | custom fusion | bytes 1574912 | tf_op jit(solution)/shard_map/jit(_take)/gather | solution.py:454
  290.7 20.6 %attend_back.1 = (bf16[512,768]{1,0:T(8,128)(2,1)S(1)}, bf16[512,768]{1,0:T(8,128)(2,1)S(1)}, bf16[512,768]{1,0:T(8,128)(2,1)S(1)}, f32[6,2,512]{2,1,0:T(2,128)S(1)}) custom-call(bf16[512,2304]{1,0:T(8,128)(2,1)S(1)} %convolution_convert_fusion.3.q_ref.k_ref.v_ref, bf16[512,2304]{1,0:T(8,128)(2,1)S(1)} %convolution_convert_fusion.3.q_ref.k_ref.v_ref, ...), custom_call_target="tpu_custom_call" | custom-call | flops 2013265920 | bytes 7077888 | tf_op jit(solution)/shard_map/attend_back/pallas_call | solution.py:254
  334.5 6.2 %fusion.33 = (f32[768]{0:T(1024)S(1)}, f32[512]{0:T(512)S(1)}, f32[512,768]{1,0:T(8,128)}) fusion(bf16[512,768]{1,0:T(8,128)(2,1)S(1)} %copy-done.15, f32[512]{0:T(512)S(1)} %add_rsqrt_fusion.1, f32[768]{0:T(1024)S(1)} %copy-done.25, bf16[512,2304]{1,0:T(8,128)(2,1)} %copy-done.22, bf16[768,2304]{1,0:T(8,128)(2,1)} %constant_dynamic-update-slice_fusion.7), kind=kOutput, calls=%fused_computation.53 | convolution fusion | flops 1814690560 | bytes 8267776 | tf_op jit(solution)/shard_map/dot_general | solution.py:482
  348.2 17.0 %collective-permute-done.11 = f32[63,128]{1,0:T(8,128)S(1)} collective-permute-done((f32[63,128]{1,0:T(8,128)S(1)}, f32[63,128]{1,0:T(8,128)S(1)}, u32[]{:S(2)}, u32[]{:S(2)}) %collective-permute-start.11) | collective-permute-done | bytes 32288 | tf_op jit(solution)/shard_map/ppermute | solution.py:311
  373.2 4.6 %all-to-all-start.4 = ((bf16[8,24,2304]{2,1,0:T(8,128)(2,1)}), bf16[8,24,2304]{2,1,0:T(8,128)(2,1)S(1)}, u32[]{:S(2)}, u32[]{:S(2)}) async-start(bf16[8,24,2304]{2,1,0:T(8,128)(2,1)} %fusion.38), calls=%async_computation.5 | async-start | bytes 1769472 | tf_op jit(solution)/shard_map/all_to_all | solution.py:347
  385.7 12.6 %collective-permute-done.14 = f32[63,128]{1,0:T(8,128)S(1)} collective-permute-done((f32[63,128]{1,0:T(8,128)S(1)}, f32[63,128]{1,0:T(8,128)S(1)}, u32[]{:S(2)}, u32[]{:S(2)}) %collective-permute-start.14) | collective-permute-done | bytes 32288 | tf_op jit(solution)/shard_map/ppermute | solution.py:311
  (163 shorter events, 96.1 us)
Async XLA Ops:
  7.2 71.1 %copy-start = (f32[768,8]{0,1:T(8,128)S(1)}, f32[768,8]{0,1:T(8,128)}, u32[]{:S(2)}) copy-start(f32[768,8]{0,1:T(8,128)} %param.24) | copy-start | bytes 73732
  7.2 33.9 %collective-permute-start = (bf16[192,2304]{1,0:T(8,128)(2,1)}, bf16[192,2304]{1,0:T(8,128)(2,1)}, u32[]{:S(2)}, u32[]{:S(2)}) collective-permute-start(bf16[192,2304]{1,0:T(8,128)(2,1)} %param.19), channel_id=1, source_target_pairs={{0,1},{1,0},{2,3},{3,2},{4,5},{5,4},{6,7},{7,6},{8,9},{9,8},{10,11... | collective-permute-start | bytes 2654216 | tf_op jit(solution)/shard_map/ppermute | solution.py:311
  7.7 30.8 %collective-permute-start.1 = (bf16[192,2304]{1,0:T(8,128)(2,1)}, bf16[192,2304]{1,0:T(8,128)(2,1)}, u32[]{:S(2)}, u32[]{:S(2)}) collective-permute-start(bf16[192,2304]{1,0:T(8,128)(2,1)} %param.19), channel_id=1, source_target_pairs={{0,2},{1,3},{2,0},{3,1},{4,6},{5,7},{6,4},{7,5},{8,10},{9,11},{10,... | collective-permute-start | bytes 2654216 | tf_op jit(solution)/shard_map/ppermute | solution.py:311
  10.3 27.2 %collective-permute-start.3 = (bf16[192,768]{1,0:T(8,128)(2,1)}, bf16[192,768]{1,0:T(8,128)(2,1)}, u32[]{:S(2)}, u32[]{:S(2)}) collective-permute-start(bf16[192,768]{1,0:T(8,128)(2,1)} %param.20), channel_id=1, source_target_pairs={{0,1},{1,0},{2,3},{3,2},{4,5},{5,4},{6,7},{7,6},{8,9},{9,8},{10,11... | collective-permute-start | bytes 884744 | tf_op jit(solution)/shard_map/ppermute | solution.py:311
  10.4 26.7 %collective-permute-start.4 = (bf16[192,768]{1,0:T(8,128)(2,1)}, bf16[192,768]{1,0:T(8,128)(2,1)}, u32[]{:S(2)}, u32[]{:S(2)}) collective-permute-start(bf16[192,768]{1,0:T(8,128)(2,1)} %param.20), channel_id=1, source_target_pairs={{0,2},{1,3},{2,0},{3,1},{4,6},{5,7},{6,4},{7,5},{8,10},{9,11},{10,... | collective-permute-start | bytes 884744 | tf_op jit(solution)/shard_map/ppermute | solution.py:311
  12.8 24.4 %copy-start.21 = (bf16[192,768]{1,0:T(8,128)(2,1)S(1)}, bf16[192,768]{1,0:T(8,128)(2,1)}, u32[]{:S(2)}) copy-start(bf16[192,768]{1,0:T(8,128)(2,1)} %param.20) | copy-start | bytes 884740
  37.2 2.9 collective-permute-start.5
  38.5 7.4 %collective-permute-start.2 = (bf16[192,2304]{1,0:T(8,128)(2,1)}, bf16[192,2304]{1,0:T(8,128)(2,1)S(1)}, u32[]{:S(2)}, u32[]{:S(2)}) collective-permute-start(bf16[192,2304]{1,0:T(8,128)(2,1)} %collective-permute-done.1), channel_id=1, source_target_pairs={{0,1},{1,0},{2,3},{3,2},{4,5},{5,4},{6,7},{7,6},{8,9},{9,8},{10,11... | collective-permute-start | bytes 2654216 | tf_op jit(solution)/shard_map/ppermute | solution.py:311
  71.7 43.8 %all-to-all-start = ((bf16[8,128,768]{2,1,0:T(8,128)(2,1)}), bf16[8,128,768]{2,1,0:T(8,128)(2,1)}, u32[]{:S(2)}, u32[]{:S(2)}) async-start(bf16[8,128,768]{2,1,0:T(8,128)(2,1)} %bitcast.81), calls=%async_computation | async-start | bytes 3145728 | tf_op jit(solution)/shard_map/all_to_all | solution.py:415
  115.4 40.9 %all-to-all-start.1 = ((bf16[8,128,768]{2,1,0:T(8,128)(2,1)}), bf16[8,128,768]{2,1,0:T(8,128)(2,1)}, u32[]{:S(2)}, u32[]{:S(2)}) async-start(bf16[8,128,768]{2,1,0:T(8,128)(2,1)} %bitcast.80), calls=%async_computation.1 | async-start | bytes 3145728 | tf_op jit(solution)/shard_map/all_to_all | solution.py:424
  119.7 169.6 %reduce-scatter.3.cloned.1.call-start = ((), (), s32[]{:S(2)}) async-start(), calls=%async_computation.8 | async-start | bytes 5898240 | tf_op jit(solution)/shard_map/reduce_scatter | solution.py:455
  229.0 40.5 %all-to-all-start.2 = ((bf16[8,128,768]{2,1,0:T(8,128)(2,1)}), bf16[8,128,768]{2,1,0:T(8,128)(2,1)}, u32[]{:S(2)}, u32[]{:S(2)}) async-start(bf16[8,128,768]{2,1,0:T(8,128)(2,1)} %bitcast.86), calls=%async_computation.2 | async-start | bytes 3145728 | tf_op jit(solution)/shard_map/all_to_all | solution.py:434
  233.3 167.4 %reduce-scatter.5.cloned.1.call-start = ((), (), s32[]{:S(2)}) async-start(), calls=%async_computation.9 | async-start | bytes 5898240 | tf_op jit(solution)/shard_map/reduce_scatter | solution.py:456
  288.4 29.1 %collective-permute-start.8 = (bf16[8,2,24,768]{3,2,1,0:T(8,128)(2,1)}, bf16[8,2,24,768]{3,2,1,0:T(8,128)(2,1)}, u32[]{:S(2)}, u32[]{:S(2)}) collective-permute-start(bf16[8,2,24,768]{3,2,1,0:T(8,128)(2,1)} %dynamic-slice_bitcast_fusion.1), channel_id=1, source_target_pairs={{0,1},{1,0},{2,3},{3,2},{4,5},{5,4},{6,7},{7,6},{8,9},{9,8},{10,11... | collective-permute-start | bytes 1769480 | tf_op jit(solution)/shard_map/ppermute | solution.py:311
  317.1 23.6 %collective-permute-start.6 = (bf16[8,2,24,2304]{3,2,1,0:T(8,128)(2,1)}, bf16[8,2,24,2304]{3,2,1,0:T(8,128)(2,1)}, u32[]{:S(2)}, u32[]{:S(2)}) collective-permute-start(bf16[8,2,24,2304]{3,2,1,0:T(8,128)(2,1)} %dynamic-slice_bitcast_fusion), channel_id=1, source_target_pairs={{0,1},{1,0},{2,3},{3,2},{4,5},{5,4},{6,7},{7,6},{8,9},{9,8},{10,11... | collective-permute-start | bytes 5308424 | tf_op jit(solution)/shard_map/ppermute | solution.py:311
  319.7 9.4 %collective-permute-start.9 = (bf16[8,1,24,768]{3,2,1,0:T(8,128)(2,1)}, bf16[8,1,24,768]{3,2,1,0:T(8,128)(2,1)}, u32[]{:S(2)}, u32[]{:S(2)}) collective-permute-start(bf16[8,1,24,768]{3,2,1,0:T(8,128)(2,1)} %constant_dynamic-slice_fusion), channel_id=1, source_target_pairs={{0,2},{1,3},{2,0},{3,1},{4,6},{5,7},{6,4},{7,5},{8,10},{9,11},{10,... | collective-permute-start | bytes 884744 | tf_op jit(solution)/shard_map/ppermute | solution.py:311
  330.8 16.7 %all-to-all-start.5 = ((bf16[8,24,768]{2,1,0:T(8,128)(2,1)}), bf16[8,24,768]{2,1,0:T(8,128)(2,1)S(1)}, u32[]{:S(2)}, u32[]{:S(2)}) async-start(bf16[8,24,768]{2,1,0:T(8,128)(2,1)} %fusion.54), calls=%async_computation.6 | async-start | bytes 589824 | tf_op jit(solution)/shard_map/all_to_all | solution.py:347
  343.6 27.2 %collective-permute-start.7 = (bf16[8,1,24,2304]{3,2,1,0:T(8,128)(2,1)}, bf16[8,1,24,2304]{3,2,1,0:T(8,128)(2,1)}, u32[]{:S(2)}, u32[]{:S(2)}) collective-permute-start(bf16[8,1,24,2304]{3,2,1,0:T(8,128)(2,1)} %constant_dynamic-slice_fusion.1), channel_id=1, source_target_pairs={{0,2},{1,3},{2,0},{3,1},{4,6},{5,7},{6,4},{7,5},{8,10},{9,11},{10,... | collective-permute-start | bytes 2654216 | tf_op jit(solution)/shard_map/ppermute | solution.py:311
  345.5 1.3 collective-permute-start.10
  346.8 18.3 %collective-permute-start.11 = (f32[63,128]{1,0:T(8,128)S(1)}, f32[63,128]{1,0:T(8,128)S(1)}, u32[]{:S(2)}, u32[]{:S(2)}) collective-permute-start(f32[63,128]{1,0:T(8,128)S(1)} %fusion.101), channel_id=1, source_target_pairs={{0,2},{1,3},{2,0},{3,1},{4,6},{5,7},{6,4},{7,5},{8,10},{9,11},{10,... | collective-permute-start | bytes 96776 | tf_op jit(solution)/shard_map/ppermute | solution.py:311
  365.1 3.9 collective-permute-start.12
  369.1 12.1 %collective-permute-start.13 = (f32[63,128]{1,0:T(8,128)S(1)}, f32[63,128]{1,0:T(8,128)S(1)}, u32[]{:S(2)}, u32[]{:S(2)}) collective-permute-start(f32[63,128]{1,0:T(8,128)S(1)} %add.243), channel_id=1, source_target_pairs={{0,8},{1,9},{2,10},{3,11},{4,12},{5,13},{6,14},{7,15},{8,0},{9,1},... | collective-permute-start | bytes 96776 | tf_op jit(solution)/shard_map/ppermute | solution.py:311
  373.2 30.5 %all-to-all-start.4 = ((bf16[8,24,2304]{2,1,0:T(8,128)(2,1)}), bf16[8,24,2304]{2,1,0:T(8,128)(2,1)S(1)}, u32[]{:S(2)}, u32[]{:S(2)}) async-start(bf16[8,24,2304]{2,1,0:T(8,128)(2,1)} %fusion.38), calls=%async_computation.5 | async-start | bytes 1769472 | tf_op jit(solution)/shard_map/all_to_all | solution.py:347
  381.2 17.2 %collective-permute-start.14 = (f32[63,128]{1,0:T(8,128)S(1)}, f32[63,128]{1,0:T(8,128)S(1)}, u32[]{:S(2)}, u32[]{:S(2)}) collective-permute-start(f32[63,128]{1,0:T(8,128)S(1)} %add.244), channel_id=1, source_target_pairs={{0,16},{1,17},{2,18},{3,19},{4,20},{5,21},{6,22},{7,23},{8,24},{9,... | collective-permute-start | bytes 96776 | tf_op jit(solution)/shard_map/ppermute | solution.py:311
  (28 other events, 125.0 us)
Sparse Core Ops, SparseCore 0:
  188.2 46.9 reduce-scatter.2
  243.0 49.0 reduce-scatter.4
